TPU v7x, 128 devices: a whole 4x4x4 slice. The times are simulated.
128 devices in a mesh: ctx: 64 (over x, z_hi, y, core), ch: 2 (over z_lo).
Axes of the slice: x: 4, y: 4, z: 4 (z_hi: 2, z_lo: 2; z = z_hi * 2 + z_lo), core: 2. Of those that a mesh axis runs over, the one named last changes fastest.
Arguments:
- tokens: bfloat16 [512, 512, 1536], P('ctx', None, 'ch'), may hold values from -6 to 6
- mix_first: bfloat16 [512, 512], replicated, may hold values from -0.25 to 0.25
- mix_second: bfloat16 [512, 512], replicated, may hold values from -0.25 to 0.25
- spectral_kernel: bfloat16 [512, 512, 1536], P('ctx', None, 'ch'), may hold values from -6 to 6
- gate_scale: float32 [1536], P('ch'), may hold values from 0.25 to 4
- up_weight: bfloat16 [4, 384, 4, 384], P('ch'), may hold values from -0.3125 to 0.3125
- down_weight: bfloat16 [4, 384, 4, 384], P('ch'), may hold values from -0.15625 to 0.15625
- first_exponents: int32 [512, 512, 12], P('ctx', None, 'ch'), may hold values from -9 to 2
- second_exponents: int32 [512, 512, 12], P(None, 'ctx', 'ch'), may hold values from -9 to 2
Outputs:
- layer_out: bfloat16 [512, 512, 1536], P('ctx', None, 'ch')
Inputs may be any that keep to these rules, and one draw needn't show every extreme that they name: `first_exponents`: power-of-two exponent of a block of 128 channels at one position. `second_exponents`: power-of-two exponent of a block of 128 channels at one position.
All inputs are finite; a program needn't handle non-finite values.
Results may differ from a plain program's by a relative error of at most 0.01.
Values may be sent and summed in bfloat16 or wider, within the bound.
No kernel may reach another device: no remote copies, remote signals or barrier semaphores. Data moves between devices by JAX's collectives and lax.ppermute only.
A program may use at most 192 MiB of HBM per device.

v0:
```python
import jax
import jax.numpy as jnp
from jax import lax
from jax.sharding import PartitionSpec as P

BLK = 128


exp_low = -9
exp_high = 3
clip_top = 448.0


def power_table(exponent, sign_of):
    result = jnp.zeros(exponent.shape, jnp.float32)
    for power_k in range(exp_low, exp_high):
        result = result + jnp.where(exponent == power_k, 2.0 ** (sign_of * power_k), 0.0).astype(
            jnp.float32
        )
    return result


def encode_blocks(values, exponent):
    shaped = values.reshape(values.shape[:-1] + (values.shape[-1] // BLK, BLK))
    encoded = jnp.clip(shaped * power_table(exponent, -1)[..., None], -clip_top, clip_top).astype(
        jnp.bfloat16
    )
    scales = power_table(exponent, 1)[..., None].astype(jnp.bfloat16)
    return (encoded, scales)


def decode_blocks(encoded, scales):
    return (encoded.astype(jnp.float32) * scales.astype(jnp.float32)).astype(jnp.bfloat16)


def expand_hidden(token_rows, up_part):
    pre_act = jnp.einsum("tic,icks->tiks", token_rows, up_part, preferred_element_type=jnp.float32)
    return jax.nn.gelu(pre_act, approximate=True).astype(jnp.bfloat16)


def body(
    tokens,
    mix_first,
    mix_second,
    spectral_kernel,
    gate_scale,
    up_weight,
    down_weight,
    first_exponents,
    second_exponents,
):
    first_mix = jnp.einsum("qr,prd->pqd", mix_first, tokens, preferred_element_type=jnp.float32)
    encoded, scales = encode_blocks(
        first_mix * spectral_kernel.astype(jnp.float32), first_exponents
    )
    arrived = decode_blocks(
        lax.all_to_all(encoded, "ctx", split_axis=1, concat_axis=0, tiled=True),
        lax.all_to_all(scales, "ctx", split_axis=1, concat_axis=0, tiled=True),
    )
    second_mix = jnp.einsum(
        "pr,rqcl->pqcl", mix_second, arrived, preferred_element_type=jnp.float32
    )
    back_encoded, back_scales = encode_blocks(
        second_mix.reshape(second_mix.shape[:2] + (-1,)), second_exponents
    )
    returned = (
        lax.all_to_all(back_encoded, "ctx", split_axis=0, concat_axis=1, tiled=True),
        lax.all_to_all(back_scales, "ctx", split_axis=0, concat_axis=1, tiled=True),
    )
    mixed_seq = decode_blocks(returned[0], returned[1]).reshape(tokens.shape)
    plain_tok = tokens.astype(jnp.float32)
    gated_seq = (
        plain_tok + mixed_seq.astype(jnp.float32) * jax.nn.sigmoid(plain_tok * gate_scale)
    ).astype(jnp.bfloat16)
    local_blocks = up_weight.shape[0]
    block_width = up_weight.shape[1]
    count_k = up_weight.shape[2]
    local_width = local_blocks * block_width
    token_rows = gated_seq.reshape(-1, local_blocks, block_width)
    share_count = count_k // lax.axis_size("ch")
    hidden = expand_hidden(token_rows, up_weight)
    partial_value = jnp.einsum(
        "tiks,isko->tko", hidden, down_weight, preferred_element_type=jnp.float32
    )
    summed = lax.psum(partial_value.astype(jnp.bfloat16), "ch").astype(jnp.float32)
    own_sum = lax.dynamic_slice_in_dim(summed, lax.axis_index("ch") * share_count, share_count, 1)
    layer_out = gated_seq.astype(jnp.float32).reshape(-1, local_width) + own_sum.reshape(
        -1, local_width
    )
    return layer_out.astype(jnp.bfloat16).reshape(tokens.shape)


def solution(mesh):
    placed = (
        P("ctx", None, "ch"),
        P(),
        P(),
        P("ctx", None, "ch"),
        P("ch"),
        P("ch", None, None, None),
        P("ch", None, None, None),
        P("ctx", None, "ch"),
        P(None, "ctx", "ch"),
    )
    return jax.shard_map(
        body, mesh=mesh, in_specs=placed, out_specs=P("ctx", None, "ch"), check_vma=False
    )
```

profile of v0, /device:TPU:1, one launch (start us, length us, event | category | flops | bytes accessed | tf_op | source)
XLA Modules:
  0.0 745.6 jit_solution(7787334942692231852)
XLA Ops:
  6.5 0.0 copy-start
  6.5 1.9 fusion.47
  8.5 0.7 copy.348
  9.2 1.8 reshape.68
  11.0 0.0 copy-start.3
  11.0 12.4 %all-to-all-start.1 = ((bf16[64,2,192]{2,1,0:T(2,128)(2,1)}), bf16[64,2,192]{2,1,0:T(2,128)(2,1)S(1)}, u32[]{:S(2)}, u32[]{:S(2)}) async-start(bf16[64,2,192]{2,1,0:T(2,128)(2,1)} %reshape.68), calls=%async_computation.1 | async-start | bytes 131072 | tf_op jit(solution)/shard_map/all_to_all | solution.py:58
  23.4 1.0 fusion.37
  24.5 2.0 copy.344
  26.5 8.6 %copy.343 = bf16[8,512,768]{1,2,0:T(8,128)(2,1)} copy(bf16[8,512,768]{2,1,0:T(8,128)(2,1)} %param.12) | data formatting | bytes 12582912 | tf_op args[3]
  35.1 0.0 copy-done.3
  35.1 10.2 %bitcast_multiply_fusion.3 = f32[8,512,768]{1,2,0:T(8,128)} fusion(bf16[8,512,768]{1,2,0:T(8,128)(2,1)} %copy.343, bf16[8,512,768]{2,1,0:T(8,128)(2,1)} %param.9, bf16[512,512]{1,0:T(8,128)(2,1)S(1)} %copy-done.3), kind=kOutput, calls=%fused_computation.29 | convolution fusion | flops 3227516928 | bytes 25690112 | tf_op jit(solution)/shard_map/qr,prd->pqd/dot_general | solution.py:52
  45.3 12.9 %copy.345 = f32[8,512,6,128]{3,0,2,1:T(8,128)} copy(f32[8,512,6,128]{1,3,2,0:T(8,128)} %bitcast.74) | data formatting | bytes 25165824 | tf_op jit(solution)/shard_map/reshape | solution.py:24
  58.2 0.0 copy-start.5
  58.2 10.4 %clamp_convert_fusion = bf16[8,512,6,128]{3,0,2,1:T(8,128)(2,1)} fusion(f32[8,512,6,128]{3,0,2,1:T(8,128)} %copy.345, f32[8,512,6]{0,2,1:T(8,128)} %copy.344), kind=kLoop, calls=%fused_computation.31 | loop fusion | flops 9437184 | bytes 18972672 | tf_op jit(solution)/shard_map/convert_element_type | solution.py:25
  68.6 0.0 all-to-all-done.1
  68.6 11.2 %all-to-all-start = ((bf16[8,512,6,128]{3,0,2,1:T(8,128)(2,1)}), bf16[8,512,6,128]{3,0,2,1:T(8,128)(2,1)}, u32[]{:S(2)}, u32[]{:S(2)}) async-start(bf16[8,512,6,128]{3,0,2,1:T(8,128)(2,1)} %clamp_convert_fusion), calls=%async_computation | async-start | bytes 12582912 | tf_op jit(solution)/shard_map/all_to_all | solution.py:57
  79.8 0.0 copy-done.5
  79.8 0.2 fusion.42
  80.1 0.7 copy.353
  80.8 0.2 fusion.46
  80.9 0.7 copy.356
  81.7 1.8 reshape.70
  83.4 1.2 reshape.69
  84.7 0.6 copy.349
  85.3 2.0 reshape.58
  87.3 3.7 copy.370
  91.1 66.8 %all-to-all-done = bf16[8,512,6,128]{3,0,2,1:T(8,128)(2,1)} async-done(((bf16[8,512,6,128]{3,0,2,1:T(8,128)(2,1)}), bf16[8,512,6,128]{3,0,2,1:T(8,128)(2,1)}, u32[]{:S(2)}, u32[]{:S(2)}) %all-to-all-start) | async-done | bytes 6291488 | tf_op jit(solution)/shard_map/all_to_all | solution.py:57
  157.8 7.6 %all-to-all-start.3 = ((bf16[64,2,192]{2,1,0:T(2,128)(2,1)}), bf16[64,2,192]{2,1,0:T(2,128)(2,1)S(1)}, u32[]{:S(2)}, u32[]{:S(2)}) async-start(bf16[64,2,192]{2,1,0:T(2,128)(2,1)} %reshape.70), calls=%async_computation.3 | async-start | bytes 131072 | tf_op jit(solution)/shard_map/all_to_all | solution.py:68
  165.5 8.9 %convert_bitcast_fusion.1 = f32[64,8,8,6,128]{4,2,0,3,1:T(8,128)} fusion(bf16[8,512,6,128]{3,0,2,1:T(8,128)(2,1)} %all-to-all-done), kind=kLoop, calls=%fused_computation.21 | loop fusion | flops 3145728 | bytes 18874368 | tf_op jit(solution)/shard_map/convert_element_type | solution.py:33
  174.4 0.0 copy-start.2
  174.4 10.9 %copy.347 = f32[64,8,8,6,128]{4,2,3,1,0:T(8,128)} copy(f32[64,8,8,6,128]{4,2,0,3,1:T(8,128)} %convert_bitcast_fusion.1) | data formatting | bytes 25165824 | tf_op jit(solution)/shard_map/convert_element_type | solution.py:33
  185.3 0.0 copy-start.4
  185.3 0.0 copy-start.7
  185.3 0.0 copy-done.2
  185.3 8.9 %fusion.21 = bf16[512,8,6,128]{3,1,2,0:T(8,128)(2,1)S(1)} fusion(f32[64,8,8,6,128]{4,2,3,1,0:T(8,128)} %copy.347, f32[512,8,6]{1,2,0:T(8,128)S(1)} %bitcast.76), kind=kLoop, calls=%fused_computation.28 | loop fusion | flops 6291456 | bytes 18972672 | tf_op jit(solution)/shard_map/convert_element_type | solution.py:33
  194.2 0.0 copy-done.4
  194.2 0.0 copy-done.7
  194.2 6.2 fusion.20
  200.4 9.2 %copy.354 = bf16[512,8,6,128]{3,1,2,0:T(8,128)(2,1)} copy(bf16[512,8,6,128]{0,3,2,1:T(8,128)(2,1)} %fusion.20) | data formatting | bytes 12582912 | tf_op jit(solution)/shard_map/convert_element_type | solution.py:25
  209.6 0.0 all-to-all-done.3
  209.6 10.5 %all-to-all-start.2 = ((bf16[512,8,6,128]{3,1,2,0:T(8,128)(2,1)}), bf16[512,8,6,128]{3,1,2,0:T(8,128)(2,1)}, u32[]{:S(2)}, u32[]{:S(2)}) async-start(bf16[512,8,6,128]{3,1,2,0:T(8,128)(2,1)} %copy.354), calls=%async_computation.2 | async-start | bytes 12582912 | tf_op jit(solution)/shard_map/all_to_all | solution.py:67
  220.2 0.0 all-reduce.2.cloned.1.call-start
  220.2 1.2 reshape.71
  221.4 0.6 copy.357
  222.0 2.0 reshape.60
  224.1 3.9 copy.371
  228.0 2.2 reshape.65
  230.2 6.1 mul.80
  236.3 0.0 copy-start.6
  236.3 12.6 %copy.360 = f32[8,512,768]{2,1,0:T(8,128)} copy(f32[8,512,768]{1,2,0:T(8,128)} %bitcast.75) | data formatting | bytes 25165824 | tf_op jit(solution)/shard_map/mul | solution.py:33
  248.9 49.4 %all-to-all-done.2 = bf16[512,8,6,128]{3,1,2,0:T(8,128)(2,1)} async-done(((bf16[512,8,6,128]{3,1,2,0:T(8,128)(2,1)}), bf16[512,8,6,128]{3,1,2,0:T(8,128)(2,1)}, u32[]{:S(2)}, u32[]{:S(2)}) %all-to-all-start.2) | async-done | bytes 6291488 | tf_op jit(solution)/shard_map/all_to_all | solution.py:67
  298.3 0.0 copy-done.6
  298.4 13.0 %fusion.22 = bf16[8,512,768]{2,1,0:T(8,128)(2,1)} fusion(bf16[8,512,768]{2,1,0:T(8,128)(2,1)} %param.9, f32[8,512,768]{2,1,0:T(8,128)} %copy.360, f32[768]{0:T(1024)S(1)} %copy-done.6, bf16[64,8,8,6,128]{4,2,3,1,0:T(8,128)(2,1)} %bitcast.24), kind=kLoop, calls=%fused_computation.32 | loop fusion | flops 37748736 | bytes 31460352 | tf_op jit(solution)/shard_map/convert_element_type | solution.py:74
  311.4 12.8 %reshape.66 = bf16[4096,2,384]{2,1,0:T(2,128)(2,1)} reshape(bf16[8,512,768]{2,1,0:T(8,128)(2,1)} %fusion.22) | data formatting | bytes 12582912 | tf_op jit(solution)/shard_map/reshape | solution.py:79
  324.2 0.0 copy-done
  324.2 39.2 %fusion.17 = bf16[4096,4,384]{2,0,1:T(8,128)(2,1)} fusion(bf16[4096,2,384,1]{2,1,0,3:T(2,128)(2,1)} %bitcast.77, bf16[2,384,4,384]{3,2,1,0:T(4,128)(2,1)S(1)} %copy-done, bf16[2,384,4,384]{3,2,1,0:T(4,128)(2,1)} %param.14), kind=kOutput, calls=%fused_computation.19 | convolution fusion | flops 19446890496 | bytes 23592960 | tf_op jit(solution)/shard_map/tiks,isko->tko/dot_general | solution.py:82
  363.3 0.0 all-reduce.2.cloned.1.call-update
  363.4 293.9 %all-reduce.2.cloned.1.call-done = bf16[4096,4,384]{2,0,1:T(8,128)(2,1)} async-done(((bf16[4096,4,384]{2,0,1:T(8,128)(2,1)}), bf16[4096,4,384]{2,0,1:T(8,128)(2,1)}) %all-reduce.2.cloned.1.call-update) | async-done | bytes 12582928 | tf_op jit(solution)/shard_map/psum | solution.py:85
  657.3 3.6 dynamic-slice_convert_fusion
  660.8 50.1 %copy.376 = f32[4096,2,384]{2,1,0:T(2,128)} copy(f32[4096,2,384]{2,0,1:T(8,128)S(1)} %dynamic-slice_convert_fusion) | data formatting | bytes 25165824 | tf_op jit(solution)/shard_map/reshape | solution.py:87
  711.0 0.0 copy-start.1
  711.0 16.8 %reshape.67 = f32[8,512,768]{2,1,0:T(8,128)} reshape(f32[4096,2,384]{2,1,0:T(2,128)} %copy.376) | data formatting | bytes 25165824 | tf_op jit(solution)/shard_map/reshape | solution.py:87
  727.7 10.5 %add_convert_fusion = bf16[8,512,768]{2,1,0:T(8,128)(2,1)} fusion(f32[8,512,768]{2,1,0:T(8,128)} %reshape.67, bf16[8,512,768]{2,1,0:T(8,128)(2,1)} %fusion.22), kind=kLoop, calls=%fused_computation.30 | loop fusion | flops 9437184 | bytes 25165824 | tf_op jit(solution)/shard_map/convert_element_type | solution.py:90
  738.3 0.0 copy-done.1
Async XLA Ops:
  6.5 317.6 %copy-start = (bf16[2,384,4,384]{3,2,1,0:T(4,128)(2,1)S(1)}, bf16[2,384,4,384]{3,2,1,0:T(4,128)(2,1)}, u32[]{:S(2)}) copy-start(bf16[2,384,4,384]{3,2,1,0:T(4,128)(2,1)} %param.15) | copy-start | bytes 7077892
  11.0 24.1 %copy-start.3 = (bf16[512,512]{1,0:T(8,128)(2,1)S(1)}, bf16[512,512]{1,0:T(8,128)(2,1)}, u32[]{:S(2)}) copy-start(bf16[512,512]{1,0:T(8,128)(2,1)} %param.10) | copy-start | bytes 1572868
  11.0 57.7 %all-to-all-start.1 = ((bf16[64,2,192]{2,1,0:T(2,128)(2,1)}), bf16[64,2,192]{2,1,0:T(2,128)(2,1)S(1)}, u32[]{:S(2)}, u32[]{:S(2)}) async-start(bf16[64,2,192]{2,1,0:T(2,128)(2,1)} %reshape.68), calls=%async_computation.1 | async-start | bytes 131072 | tf_op jit(solution)/shard_map/all_to_all | solution.py:58
  58.2 21.6 %copy-start.5 = (s32[512,8,6]{0,1,2:T(8,128)S(1)}, s32[512,8,6]{0,1,2:T(8,128)}, u32[]{:S(2)}) copy-start(s32[512,8,6]{0,1,2:T(8,128)} %param.17) | copy-start | bytes 294916
  68.6 89.2 %all-to-all-start = ((bf16[8,512,6,128]{3,0,2,1:T(8,128)(2,1)}), bf16[8,512,6,128]{3,0,2,1:T(8,128)(2,1)}, u32[]{:S(2)}, u32[]{:S(2)}) async-start(bf16[8,512,6,128]{3,0,2,1:T(8,128)(2,1)} %clamp_convert_fusion), calls=%async_computation | async-start | bytes 12582912 | tf_op jit(solution)/shard_map/all_to_all | solution.py:57
  157.8 51.8 %all-to-all-start.3 = ((bf16[64,2,192]{2,1,0:T(2,128)(2,1)}), bf16[64,2,192]{2,1,0:T(2,128)(2,1)S(1)}, u32[]{:S(2)}, u32[]{:S(2)}) async-start(bf16[64,2,192]{2,1,0:T(2,128)(2,1)} %reshape.70), calls=%async_computation.3 | async-start | bytes 131072 | tf_op jit(solution)/shard_map/all_to_all | solution.py:68
  174.4 10.9 %copy-start.2 = (f32[64,8,8,6,1]{2,3,1,0,4:T(8,128)S(1)}, f32[64,8,8,6,1]{2,3,1,0,4:T(8,128)}, u32[]{:S(2)}) copy-start(f32[64,8,8,6,1]{2,3,1,0,4:T(8,128)} %copy.370) | copy-start | bytes 294916
  185.3 8.9 %copy-start.4 = (f32[512,8,6]{0,2,1:T(8,128)S(1)}, f32[512,8,6]{0,2,1:T(8,128)}, u32[]{:S(2)}) copy-start(f32[512,8,6]{0,2,1:T(8,128)} %copy.353) | copy-start | bytes 294916
  185.3 8.9 %copy-start.7 = (bf16[512,512]{1,0:T(8,128)(2,1)S(1)}, bf16[512,512]{1,0:T(8,128)(2,1)}, u32[]{:S(2)}) copy-start(bf16[512,512]{1,0:T(8,128)(2,1)} %param.11) | copy-start | bytes 1572868
  209.6 88.7 %all-to-all-start.2 = ((bf16[512,8,6,128]{3,1,2,0:T(8,128)(2,1)}), bf16[512,8,6,128]{3,1,2,0:T(8,128)(2,1)}, u32[]{:S(2)}, u32[]{:S(2)}) async-start(bf16[512,8,6,128]{3,1,2,0:T(8,128)(2,1)} %copy.354), calls=%async_computation.2 | async-start | bytes 12582912 | tf_op jit(solution)/shard_map/all_to_all | solution.py:67
  220.2 437.1 %all-reduce.2.cloned.1.call-start = ((), (), s32[]{:S(2)}) async-start(), calls=%async_computation.4 | async-start | bytes 25165824 | tf_op jit(solution)/shard_map/psum | solution.py:85
  236.3 62.0 %copy-start.6 = (f32[768]{0:T(1024)S(1)}, f32[768]{0:T(1024)}, u32[]{:S(2)}) copy-start(f32[768]{0:T(1024)} %param.13) | copy-start | bytes 9220
  711.0 27.3 %copy-start.1 = (bf16[2,384,4,384]{3,2,1,0:T(4,128)(2,1)S(1)}, bf16[2,384,4,384]{3,2,1,0:T(4,128)(2,1)}, u32[]{:S(2)}) copy-start(bf16[2,384,4,384]{3,2,1,0:T(4,128)(2,1)} %param.15) | copy-start | bytes 7077892
Sparse Core Ops, SparseCore 0:
  363.5 293.7 all-reduce.1
where the time goes:
time: 753 us; the launch traced here: 746 us
  waiting for transfers between devices  410 us (54%)
  local copies, waits for them, and re-layouts  165 us (22%)
  other arithmetic  58.8 us (8%)
  matrix products  55.6 us (7%)
  starting transfers between devices  41.8 us (6%)
  between operations  14 us (2%)
    psum x1, waiting for transfers between devices, body(): lax.psum(partial_value.astype(jnp.bfloat16), 'ch').astype(jnp.float32)  294 us
    reshape x2, local copies, waits for them, and re-layouts, body(): own_sum.reshape(-1, local_width)  66.9 us
    all_to_all x1, waiting for transfers between devices, body(): lax.all_to_all(encoded, 'ctx', split_axis=1, concat_axis=0, tiled=True)  66.8 us
    all_to_all x1, waiting for transfers between devices, body(): lax.all_to_all(back_encoded, 'ctx', split_axis=0, concat_axis=1, tiled=True)  49.4 us
    dot_general x1, matrix products, body(): jnp.einsum('tiks,isko->tko', hidden, down_weight, preferred_element_type=...  39.2 us
    mul x2, local copies, waits for them, and re-layouts, decode_blocks(): encoded.astype(jnp.float32) * scales.astype(jnp.float32)  18.7 us
  transfers between devices with their start and end apart: 5, of which 3 were waited for; matrix products, arithmetic and copies ran while one was open for 17% of the time, Pallas kernels for 0%

commit v1 on v0

v1 whole, which is shorter than its diff:
```python
import functools

import jax
import jax.numpy as jnp
import numpy as np
from jax import lax
from jax.experimental import pallas as pl
from jax.experimental.pallas import tpu as pltpu
from jax.sharding import PartitionSpec as P

BLK = 128
HALF = 768
BW = 384
WIDE = 1536
VMEM = 56 * 1024 * 1024
BOTH = ("ctx", "ch")


def limits(exponent):
    return lax.shift_left(jnp.ones_like(exponent), exponent + 9).astype(jnp.float32) * 0.875


def regroup_matrix():
    matrix = np.zeros((256, 256), np.float32)
    for r in range(4):
        for j in range(8):
            for a in range(8):
                matrix[r * 64 + j * 8 + a, a * 32 + j * 4 + r] = 1.0
    return matrix


def first_kernel(mix_ref, perm_ref, tok_ref, spec_ref, exp_ref, out0_ref, out1_ref, enc_ref):
    columns = limits(exp_ref[0]).T
    mix = mix_ref[...]
    for pair in range(4):
        rhs = jnp.concatenate([tok_ref[2 * pair], tok_ref[2 * pair + 1]], axis=1)
        acc = jnp.dot(mix, rhs, preferred_element_type=jnp.float32)
        for side in range(2):
            a = 2 * pair + side
            value = acc[:, side * BLK:(side + 1) * BLK] * spec_ref[a].astype(jnp.float32)
            top = columns[:, a:a + 1]
            enc_ref[a] = jnp.clip(value, -top, top).astype(jnp.bfloat16)

    def regroup(g, carry):
        rows = pl.ds(pl.multiple_of(g * 32, 32), 32)
        both = jnp.concatenate(
            [enc_ref[:, rows, :].reshape(256, BLK), tok_ref[:, rows, :].reshape(256, BLK)], axis=1
        )
        moved = jnp.dot(perm_ref[...], both, preferred_element_type=jnp.float32)
        dest = pl.ds(pl.multiple_of(g * 8, 8), 8)
        for r in range(4):
            out_ref = (out0_ref, out1_ref)[r // 2]
            part = moved[r * 64:(r + 1) * 64]
            for t in range(2):
                out_ref[dest, r % 2, t] = (
                    part[:, t * BLK:(t + 1) * BLK].reshape(8, 8, BLK).astype(jnp.bfloat16)
                )
        return carry

    lax.fori_loop(0, 16, regroup, 0, unroll=4)


def first_stage(mix_first, perm, tokens, spectral, exponents):
    out = jax.ShapeDtypeStruct((128, 2, 2, 8, HALF), jnp.bfloat16)
    out_spec = pl.BlockSpec((128, 2, 2, 8, BLK), lambda d: (0, 0, 0, 0, d))
    wide = pl.BlockSpec((8, 512, BLK), lambda d: (0, 0, d))
    return pl.pallas_call(
        first_kernel,
        grid=(HALF // BLK,),
        in_specs=[
            pl.BlockSpec((512, 512), lambda d: (0, 0)),
            pl.BlockSpec((256, 256), lambda d: (0, 0)),
            wide,
            wide,
            pl.BlockSpec((1, 8, 512), lambda d: (d, 0, 0)),
        ],
        out_specs=[out_spec, out_spec],
        out_shape=[out, out],
        scratch_shapes=[pltpu.VMEM((8, 512, BLK), jnp.bfloat16)],
        compiler_params=pltpu.CompilerParams(vmem_limit_bytes=VMEM),
        cost_estimate=pl.CostEstimate(flops=6_400_000_000, bytes_accessed=25_200_000, transcendentals=0),
        name="first_mix",
    )(mix_first, perm, tokens, spectral, exponents)


def mixer_kernel(mix_ref, recv_ref, top_ref, gate_ref, up_ref, down_ref, out_ref, gated_ref):
    m = pl.program_id(1)
    lead = pl.ds(pl.multiple_of(m * 32, 32), 32)
    for c in range(2):
        right = recv_ref[:, c, 0, 0].reshape(512, HALF)
        mixed = jnp.dot(mix_ref[...], right, preferred_element_type=jnp.float32)
        tok = recv_ref[lead, c, 0, 1].reshape(256, HALF).astype(jnp.float32)
        slope = jax.nn.sigmoid(tok * gate_ref[c:c + 1, :])
        for n in range(6):
            cols = slice(n * BLK, (n + 1) * BLK)
            top = top_ref[0, :, c * 6 + n:c * 6 + n + 1]
            held = jnp.clip(mixed[:, cols], -top, top).astype(jnp.bfloat16).astype(jnp.float32)
            gated_ref[:, c * HALF + n * BLK:c * HALF + (n + 1) * BLK] = (
                tok[:, cols] + held * slope[:, cols]
            ).astype(jnp.bfloat16)
    totals = [None] * 4
    for i in range(4):
        pre = jnp.dot(
            gated_ref[:, i * BW:(i + 1) * BW], up_ref[i], preferred_element_type=jnp.float32
        )
        hidden = jax.nn.gelu(pre, approximate=True).astype(jnp.bfloat16)
        for k in range(4):
            cols = slice(k * BW, (k + 1) * BW)
            part = jnp.dot(hidden[:, cols], down_ref[i, :, cols], preferred_element_type=jnp.float32)
            totals[k] = part if i == 0 else totals[k] + part
    for k in range(4):
        result = (gated_ref[:, k * BW:(k + 1) * BW].astype(jnp.float32) + totals[k]).astype(jnp.bfloat16)
        out_ref[:, k // 2, 0, :, (k % 2) * BW:(k % 2 + 1) * BW] = result.reshape(32, 8, BW)


def mixer_stage(mix_second, received, tops, gate, up, down):
    fixed = pl.BlockSpec((4, BW, WIDE), lambda q, m: (0, 0, 0))
    return pl.pallas_call(
        mixer_kernel,
        grid=(2, 2),
        in_specs=[
            pl.BlockSpec((256, 512), lambda q, m: (m, 0)),
            pl.BlockSpec((64, 2, 1, 2, 8, HALF), lambda q, m: (0, 0, q, 0, 0, 0)),
            pl.BlockSpec((1, 256, 12), lambda q, m: (q, m, 0)),
            pl.BlockSpec((2, HALF), lambda q, m: (0, 0)),
            fixed,
            fixed,
        ],
        out_specs=pl.BlockSpec((32, 2, 1, 8, HALF), lambda q, m: (m, 0, q, 0, 0)),
        out_shape=jax.ShapeDtypeStruct((64, 2, 2, 8, HALF), jnp.bfloat16),
        scratch_shapes=[pltpu.VMEM((256, WIDE), jnp.bfloat16)],
        compiler_params=pltpu.CompilerParams(vmem_limit_bytes=VMEM),
        cost_estimate=pl.CostEstimate(
            flops=12_000_000_000, bytes_accessed=19_000_000, transcendentals=8_000_000
        ),
        name="second_mix_and_channel_mix",
    )(mix_second, received, tops, gate, up, down)


def last_kernel(perm_ref, in0_ref, in1_ref, out_ref):
    def regroup(g, carry):
        parts = []
        for u in range(2):
            source = pl.ds(pl.multiple_of(g * 16 + u * 8, 8), 8)
            rows = [(in0_ref, in1_ref)[r // 2][source, r % 2].reshape(64, BLK) for r in range(4)]
            parts.append(jnp.concatenate(rows, axis=0))
        moved = jnp.dot(perm_ref[...], jnp.concatenate(parts, axis=1), preferred_element_type=jnp.float32)
        for u in range(2):
            dest = pl.ds(pl.multiple_of(g * 64 + u * 32, 32), 32)
            out_ref[:, dest, :] = (
                moved[:, u * BLK:(u + 1) * BLK].reshape(8, 32, BLK).astype(jnp.bfloat16)
            )
        return carry

    lax.fori_loop(0, 8, regroup, 0, unroll=4)


def last_stage(perm, part0, part1):
    block = pl.BlockSpec((128, 2, 8, BLK), lambda d: (0, 0, 0, d))
    return pl.pallas_call(
        last_kernel,
        grid=(HALF // BLK,),
        in_specs=[pl.BlockSpec((256, 256), lambda d: (0, 0)), block, block],
        out_specs=pl.BlockSpec((8, 512, BLK), lambda d: (0, 0, d)),
        out_shape=jax.ShapeDtypeStruct((8, 512, HALF), jnp.bfloat16),
        compiler_params=pltpu.CompilerParams(vmem_limit_bytes=VMEM),
        cost_estimate=pl.CostEstimate(flops=1_600_000_000, bytes_accessed=12_600_000, transcendentals=0),
        name="regroup_result",
    )(perm, part0, part1)


def swap(value):
    return lax.ppermute(value, "ch", [(0, 1), (1, 0)])


def whole_weight(weight, ch):
    rows = weight.shape[0] * weight.shape[1]
    size = lax.axis_size("ctx")
    flat = weight.reshape(rows, weight.shape[2] * weight.shape[3])
    piece = rows // size
    start = lax.axis_index("ctx") * piece
    mine = lax.dynamic_slice_in_dim(weight.reshape(rows, 4, BW), start, piece, 0).reshape(piece, -1)
    other = lax.all_gather(swap(mine), "ctx", axis=0, tiled=True)
    low = jnp.where(ch == 0, flat, other)
    high = jnp.where(ch == 0, other, flat)
    return jnp.concatenate([low, high], axis=0).reshape(4, BW, WIDE)


def body(
    tokens,
    mix_first,
    mix_second,
    spectral_kernel,
    gate_scale,
    up_weight,
    down_weight,
    first_exponents,
    second_exponents,
):
    ch = lax.axis_index("ch")
    perm = regroup_matrix()
    send0, send1 = first_stage(
        mix_first,
        jnp.asarray(perm, jnp.bfloat16),
        tokens,
        spectral_kernel,
        first_exponents.transpose(2, 0, 1),
    )
    exchange = functools.partial(
        lax.all_to_all, axis_name=BOTH, split_axis=0, concat_axis=0, tiled=True
    )
    up = whole_weight(up_weight, ch)
    down = whole_weight(down_weight, ch)
    own_gate = gate_scale.reshape(1, HALF)
    other_gate = swap(own_gate)
    gate = jnp.where(
        ch == 0,
        jnp.concatenate([own_gate, other_gate], axis=0),
        jnp.concatenate([other_gate, own_gate], axis=0),
    )
    columns = second_exponents.transpose(2, 1, 0)
    mine = lax.dynamic_slice_in_dim(columns, 4 * ch, 4, 1)
    other = swap(lax.dynamic_slice_in_dim(columns, 4 * (1 - ch), 4, 1))
    exps = jnp.where(
        ch == 0, jnp.concatenate([mine, other], axis=0), jnp.concatenate([other, mine], axis=0)
    )
    tops = limits(exps.transpose(1, 2, 0))
    back = []
    for h, send in enumerate((send0, send1)):
        received = exchange(send).reshape(64, 2, 2, 2, 8, HALF)
        mixed = mixer_stage(mix_second, received, tops[2 * h:2 * h + 2], gate, up, down)
        back.append(exchange(mixed.reshape(128, 2, 8, HALF)))
    return last_stage(jnp.asarray(perm.T, jnp.bfloat16), back[0], back[1])


def solution(mesh):
    placed = (
        P("ctx", None, "ch"),
        P(),
        P(),
        P("ctx", None, "ch"),
        P("ch"),
        P("ch", None, None, None),
        P("ch", None, None, None),
        P("ctx", None, "ch"),
        P(None, "ctx", "ch"),
    )
    return jax.shard_map(
        body, mesh=mesh, in_specs=placed, out_specs=P("ctx", None, "ch"), check_vma=False
    )
```

time: 753 us -> 445 us (0.59)
  waiting for transfers between devices: 410 us -> 245 us
  local copies, waits for them, and re-layouts: 165 us -> 22.2 us
  Pallas kernels: 0 us -> 75.8 us
  matrix products: 55.6 us -> 0 us
  other arithmetic: 58.8 us -> 9.83 us
  blocking collectives: 0 us -> 47.1 us
  starting transfers between devices: 41.8 us -> 30.3 us
    psum x1 -> x0, waiting for transfers between devices: 294 us -> none  [body(): lax.psum(partial_value.astype(jnp.bfloat16), 'ch').astype(jnp.float32)]
    ppermute x0 -> x4, waiting for transfers between devices: none -> 133 us  [swap(): return lax.ppermute(value, 'ch', [(0, 1), (1, 0)])]
    reshape x4 -> x1, local copies, waits for them, and re-layouts: 92.6 us -> 0.01 us  [body(): own_gate = gate_scale.reshape(1, HALF)]
    all_to_all x4 -> x3, waiting for transfers between devices: 116 us -> 32.3 us  [the longest x1 17 us: body(): back.append(exchange(mixed.reshape(128, 2, 8, HALF)))]
    all_gather x0 -> x2, waiting for transfers between devices: none -> 79.7 us  [whole_weight(): other = lax.all_gather(swap(mine), 'ctx', axis=0, tiled=True)]
    pallas_call x0 -> x4, Pallas kernels: none -> 75.8 us  [the longest x2 50.5 us: mixer_stage(): pl.pallas_call(mixer_kernel, grid=(2, 2), in_specs=[pl.BlockSpec((256, 51...]
    convert_element_type x8 -> x0, other arithmetic: 57.5 us -> none  [the longest x1 13 us: body(): gated_seq = (plain_tok + mixed_seq.astype(jnp.float32) * jax.nn.sigmoid(p...]
    dot_general x3 -> x0, matrix products: 55.6 us -> none  [the longest x1 39.2 us: body(): jnp.einsum('tiks,isko->tko', hidden, down_weight, preferred_element_type=...]
  transfers between devices with their start and end apart: 5 -> 9, of which waited for: 3 -> 8; matrix products, arithmetic and copies ran while one was open for 17% -> 7% of each run, Pallas kernels for 0% -> 15%
where the time goes in v1:
time: 445 us; the launch traced here: 444 us
  waiting for transfers between devices  245 us (55%)
  Pallas kernels  75.8 us (17%)
  blocking collectives  47.1 us (11%)
  starting transfers between devices  30.3 us (7%)
  local copies, waits for them, and re-layouts  22.2 us (5%)
  between operations  13.5 us (3%)
  other arithmetic  9.83 us (2%)
    ppermute x4, waiting for transfers between devices, swap(): return lax.ppermute(value, 'ch', [(0, 1), (1, 0)])  133 us
    all_gather x2, waiting for transfers between devices, whole_weight(): other = lax.all_gather(swap(mine), 'ctx', axis=0, tiled=True)  79.7 us
    pallas_call x2, Pallas kernels, mixer_stage(): pl.pallas_call(mixer_kernel, grid=(2, 2), in_specs=[pl.BlockSpec((256, 51...  50.5 us
    all_to_all x1, blocking collectives, body(): back.append(exchange(mixed.reshape(128, 2, 8, HALF)))  47.1 us
    all_to_all x2, starting transfers between devices, body(): received = exchange(send).reshape(64, 2, 2, 2, 8, HALF)  19.9 us
    unnamed x18, local copies, waits for them, and re-layouts  17 us
    all_to_all x1, waiting for transfers between devices, body(): back.append(exchange(mixed.reshape(128, 2, 8, HALF)))  17 us
    pallas_call x1, Pallas kernels, first_stage(): pl.pallas_call(first_kernel, grid=(HALF // BLK,), in_specs=[pl.BlockSpec(...  16.9 us
  transfers between devices with their start and end apart: 9, of which 8 were waited for; matrix products, arithmetic and copies ran while one was open for 7% of the time, Pallas kernels for 15%

profile of v1, /device:TPU:1, one launch (start us, length us, event | category | flops | bytes accessed | tf_op | source)
XLA Modules:
  0.0 443.9 jit_solution(18061214837463435117)
XLA Ops:
  6.5 0.0 all-gather.7.cloned.1.call-start
  6.5 0.8 constant_dynamic-slice_fusion
  7.4 2.5 collective-permute-start.3
  9.9 1.5 collective-permute-done.3
  11.4 0.0 copy-start.2
  11.4 0.6 copy-done.2
  12.0 0.0 all-gather.7.cloned.1.call-update
  12.0 16.9 %first_mix.1 = (bf16[128,2,2,8,768]{4,3,2,1,0:T(8,128)(2,1)}, bf16[128,2,2,8,768]{4,3,2,1,0:T(8,128)(2,1)}) custom-call(bf16[512,512]{1,0:T(8,128)(2,1)} %mix_ref.3, bf16[256,256]{1,0:T(8,128)(2,1)} %constant.29.clone.perm_ref, bf16[8,512,768]{2,1,0:T(8,128)(2,1)} %tok_ref.1, bf16[8,512,768]{2,1,0:T(8,128)(2,1)} %spec_ref.1, s32[6,8,512]{2,1,0:T(8,128)} %bitcast.47), custom_call_target="tpu_custom_call" | custom-call | flops 6400000000 | bytes 25200000 | tf_op jit(solution)/shard_map/first_mix/pallas_call | solution.py:67
  28.9 12.1 %all-to-all-start = ((bf16[128,2,2,8,768]{4,3,2,1,0:T(8,128)(2,1)}), bf16[128,2,2,8,768]{4,3,2,1,0:T(8,128)(2,1)}, u32[]{:S(2)}, u32[]{:S(2)}) async-start(bf16[128,2,2,8,768]{4,3,2,1,0:T(8,128)(2,1)} %get-tuple-element.7), calls=%async_computation | async-start | bytes 12582912 | tf_op jit(solution)/shard_map/all_to_all | solution.py:230
  41.0 0.0 all-gather.5.cloned.1.call-start
  41.0 0.8 constant_dynamic-slice_fusion.1
  41.9 1.6 collective-permute-start.2
  43.5 62.5 %collective-permute-done.2 = bf16[12,1536]{1,0:T(8,128)(2,1)S(1)} collective-permute-done((bf16[12,1536]{1,0:T(8,128)(2,1)S(1)}, bf16[12,1536]{1,0:T(8,128)(2,1)S(1)}, u32[]{:S(2)}, u32[]{:S(2)}) %collective-permute-start.2) | collective-permute-done | bytes 36896 | tf_op jit(solution)/shard_map/ppermute | solution.py:173
  106.0 0.0 copy-start.3
  106.0 0.6 copy-done.3
  106.6 0.0 all-gather.5.cloned.1.call-update
  106.6 15.3 %all-to-all-done = bf16[128,2,2,8,768]{4,3,2,1,0:T(8,128)(2,1)} async-done(((bf16[128,2,2,8,768]{4,3,2,1,0:T(8,128)(2,1)}), bf16[128,2,2,8,768]{4,3,2,1,0:T(8,128)(2,1)}, u32[]{:S(2)}, u32[]{:S(2)}) %all-to-all-start) | async-done | bytes 6291488 | tf_op jit(solution)/shard_map/all_to_all | solution.py:230
  122.0 0.0 copy-start.4
  122.0 0.0 copy-start.1
  122.0 7.9 %all-to-all-start.2 = ((bf16[128,2,2,8,768]{4,3,2,1,0:T(8,128)(2,1)}), bf16[128,2,2,8,768]{4,3,2,1,0:T(8,128)(2,1)}, u32[]{:S(2)}, u32[]{:S(2)}) async-start(bf16[128,2,2,8,768]{4,3,2,1,0:T(8,128)(2,1)} %get-tuple-element.8), calls=%async_computation.2 | async-start | bytes 12582912 | tf_op jit(solution)/shard_map/all_to_all | solution.py:230
  129.8 0.0 copy-done.4
  129.9 1.6 collective-permute-start.1
  131.5 0.0 copy-done.1
  131.5 0.1 collective-permute-start
  131.6 2.4 copy.24
  134.0 3.6 copy.22
  137.6 60.8 %collective-permute-done.1 = f32[1,768]{1,0:T(1,128)S(1)} collective-permute-done((f32[1,768]{1,0:T(1,128)S(1)}, f32[1,768]{1,0:T(1,128)S(1)}, u32[]{:S(2)}, u32[]{:S(2)}) %collective-permute-start.1) | collective-permute-done | bytes 3104 | tf_op jit(solution)/shard_map/ppermute | solution.py:173
  198.3 0.6 maximum_select_fusion.gate_ref
  198.9 8.3 %collective-permute-done = s32[6,4,512]{2,1,0:T(4,128)S(1)} collective-permute-done((s32[6,4,512]{2,1,0:T(4,128)S(1)}, s32[6,4,512]{2,1,0:T(4,128)S(1)}, u32[]{:S(2)}, u32[]{:S(2)}) %collective-permute-start) | collective-permute-done | bytes 49184 | tf_op jit(solution)/shard_map/ppermute | solution.py:173
  207.2 0.7 pad_add_fusion.1
  207.9 1.2 copy.18
  209.2 1.3 copy.19
  210.5 0.2 multiply_bitcast_fusion
  210.7 1.0 fusion
  211.7 14.3 %all-gather.7.cloned.1.call-done = bf16[64,12,1536]{2,1,0:T(8,128)(2,1)} async-done(((bf16[1,12,1536]{2,1,0:T(8,128)(2,1)}), bf16[64,12,1536]{2,1,0:T(8,128)(2,1)}) %all-gather.7.cloned.1.call-update) | async-done | bytes 2359312 | tf_op jit(solution)/shard_map/all_gather | solution.py:183
  226.0 4.9 %reshape.55 = bf16[768,1536]{1,0:T(8,128)(2,1)} reshape(bf16[64,12,1536]{2,1,0:T(8,128)(2,1)} %all-gather.7.cloned.1.call-done) | data formatting | bytes 4718592
  230.9 65.4 %all-gather.5.cloned.1.call-done = bf16[64,12,1536]{2,1,0:T(8,128)(2,1)} async-done(((bf16[1,12,1536]{2,1,0:T(8,128)(2,1)}), bf16[64,12,1536]{2,1,0:T(8,128)(2,1)}) %all-gather.5.cloned.1.call-update) | async-done | bytes 2359312 | tf_op jit(solution)/shard_map/all_gather | solution.py:183
  296.3 4.9 %reshape.53 = bf16[768,1536]{1,0:T(8,128)(2,1)} reshape(bf16[64,12,1536]{2,1,0:T(8,128)(2,1)} %all-gather.5.cloned.1.call-done) | data formatting | bytes 4718592
  301.2 3.4 broadcast_select_fusion.1
  304.6 2.5 pad_maximum_fusion
  307.1 2.5 pad_maximum_fusion.1
  309.6 25.2 %second_mix_and_channel_mix.2 = bf16[64,2,2,8,768]{4,3,2,1,0:T(8,128)(2,1)} custom-call(bf16[512,512]{1,0:T(8,128)(2,1)} %mix_ref.5, bf16[64,2,2,2,8,768]{5,4,3,2,1,0:T(8,128)(2,1)} %bitcast.1.recv_ref, f32[2,512,12]{2,1,0:T(8,128)} %get-tuple-element.14.top_ref, f32[2,768]{1,0:T(2,128)} %maximum_select_fusion.gate_ref, bf16[4,384,1536]{2,1,0:T(8,128)(2,1)} %bitcast.31, ...), custom_call_target="tpu_custom_call" | custom-call | flops 12000000000 | bytes 19000000 | tf_op jit(solution)/shard_map/second_mix_and_channel_mix/pallas_call | solution.py:118
  334.8 0.0 all-to-all-done.2
  334.8 4.5 %all-to-all-start.1 = ((bf16[128,2,8,768]{3,2,1,0:T(8,128)(2,1)}), bf16[128,2,8,768]{3,2,1,0:T(8,128)(2,1)S(1)}, u32[]{:S(2)}, u32[]{:S(2)}) async-start(bf16[128,2,8,768]{3,2,1,0:T(8,128)(2,1)} %bitcast.35), calls=%async_computation.1 | async-start | bytes 6291456 | tf_op jit(solution)/shard_map/all_to_all | solution.py:232
  339.4 25.3 %second_mix_and_channel_mix.3 = bf16[64,2,2,8,768]{4,3,2,1,0:T(8,128)(2,1)} custom-call(bf16[512,512]{1,0:T(8,128)(2,1)} %mix_ref.5, bf16[64,2,2,2,8,768]{5,4,3,2,1,0:T(8,128)(2,1)} %bitcast.12.recv_ref, f32[2,512,12]{2,1,0:T(8,128)} %get-tuple-element.13.top_ref, f32[2,768]{1,0:T(2,128)} %maximum_select_fusion.gate_ref, bf16[4,384,1536]{2,1,0:T(8,128)(2,1)} %bitcast.32, ...), custom_call_target="tpu_custom_call" | custom-call | flops 12000000000 | bytes 19000000 | tf_op jit(solution)/shard_map/second_mix_and_channel_mix/pallas_call | solution.py:118
  364.7 17.0 %all-to-all-done.1.in0_ref = bf16[128,2,8,768]{3,2,1,0:T(8,128)(2,1)S(1)} async-done(((bf16[128,2,8,768]{3,2,1,0:T(8,128)(2,1)}), bf16[128,2,8,768]{3,2,1,0:T(8,128)(2,1)S(1)}, u32[]{:S(2)}, u32[]{:S(2)}) %all-to-all-start.1) | async-done | bytes 3145760 | tf_op jit(solution)/shard_map/all_to_all | solution.py:232
  381.6 0.0 copy-start
  381.6 47.1 %all_to_all.20.in1_ref = bf16[128,2,8,768]{3,2,1,0:T(8,128)(2,1)} all-to-all(bf16[128,2,8,768]{3,2,1,0:T(8,128)(2,1)} %bitcast.36), channel_id=1, replica_groups=mesh['ctx'=64,'ch'=2] {'ctx','ch'}, dimensions={0} | all-to-all | bytes 6291456 | tf_op jit(solution)/shard_map/all_to_all | solution.py:232
  428.7 0.0 copy-done
  428.7 8.3 %regroup_result.1 = bf16[8,512,768]{2,1,0:T(8,128)(2,1)} custom-call(bf16[256,256]{1,0:T(8,128)(2,1)} %constant.30.clone.perm_ref, bf16[128,2,8,768]{3,2,1,0:T(8,128)(2,1)} %copy-done, bf16[128,2,8,768]{3,2,1,0:T(8,128)(2,1)} %all_to_all.20.in1_ref), custom_call_target="tpu_custom_call" | custom-call | flops 1600000000 | bytes 12600000 | tf_op jit(solution)/shard_map/regroup_result/pallas_call | solution.py:160
  (6 shorter events, 0.1 us)
Async XLA Ops:
  6.5 219.5 %all-gather.7.cloned.1.call-start = ((), (), s32[]{:S(2)}) async-start(), calls=%async_computation.5 | async-start | bytes 3194880 | tf_op jit(solution)/shard_map/all_gather | solution.py:183
  7.4 4.0 collective-permute-start.3
  11.4 0.6 copy-start.2
  28.9 93.0 %all-to-all-start = ((bf16[128,2,2,8,768]{4,3,2,1,0:T(8,128)(2,1)}), bf16[128,2,2,8,768]{4,3,2,1,0:T(8,128)(2,1)}, u32[]{:S(2)}, u32[]{:S(2)}) async-start(bf16[128,2,2,8,768]{4,3,2,1,0:T(8,128)(2,1)} %get-tuple-element.7), calls=%async_computation | async-start | bytes 12582912 | tf_op jit(solution)/shard_map/all_to_all | solution.py:230
  41.0 255.3 %all-gather.5.cloned.1.call-start = ((), (), s32[]{:S(2)}) async-start(), calls=%async_computation.4 | async-start | bytes 3194880 | tf_op jit(solution)/shard_map/all_gather | solution.py:183
  41.9 64.1 %collective-permute-start.2 = (bf16[12,1536]{1,0:T(8,128)(2,1)S(1)}, bf16[12,1536]{1,0:T(8,128)(2,1)S(1)}, u32[]{:S(2)}, u32[]{:S(2)}) collective-permute-start(bf16[12,1536]{1,0:T(8,128)(2,1)S(1)} %bitcast.46), channel_id=1, source_target_pairs={{0,1},{1,0},{2,3},{3,2},{4,5},{5,4},{6,7},{7,6},{8,9},{9,8},{10,11... | collective-permute-start | bytes 110600 | tf_op jit(solution)/shard_map/ppermute | solution.py:173
  106.0 0.6 copy-start.3
  122.0 7.9 %copy-start.4 = (f32[768]{0:T(1024)S(1)}, f32[768]{0:T(1024)}, u32[]{:S(2)}) copy-start(f32[768]{0:T(1024)} %param.15) | copy-start | bytes 9220
  122.0 9.5 %copy-start.1 = (s32[512,8,6]{0,1,2:T(8,128)S(1)}, s32[512,8,6]{0,1,2:T(8,128)}, u32[]{:S(2)}) copy-start(s32[512,8,6]{0,1,2:T(8,128)} %param.19) | copy-start | bytes 294916
  122.0 212.9 %all-to-all-start.2 = ((bf16[128,2,2,8,768]{4,3,2,1,0:T(8,128)(2,1)}), bf16[128,2,2,8,768]{4,3,2,1,0:T(8,128)(2,1)}, u32[]{:S(2)}, u32[]{:S(2)}) async-start(bf16[128,2,2,8,768]{4,3,2,1,0:T(8,128)(2,1)} %get-tuple-element.8), calls=%async_computation.2 | async-start | bytes 12582912 | tf_op jit(solution)/shard_map/all_to_all | solution.py:230
  129.9 68.5 %collective-permute-start.1 = (f32[1,768]{1,0:T(1,128)S(1)}, f32[1,768]{1,0:T(1,128)S(1)}, u32[]{:S(2)}, u32[]{:S(2)}) collective-permute-start(f32[1,768]{1,0:T(1,128)S(1)} %reshape.40), channel_id=1, source_target_pairs={{0,1},{1,0},{2,3},{3,2},{4,5},{5,4},{6,7},{7,6},{8,9},{9,8},{10,11... | collective-permute-start | bytes 9224 | tf_op jit(solution)/shard_map/ppermute | solution.py:173
  131.5 75.8 %collective-permute-start = (s32[6,4,512]{2,1,0:T(4,128)S(1)}, s32[6,4,512]{2,1,0:T(4,128)S(1)}, u32[]{:S(2)}, u32[]{:S(2)}) collective-permute-start(s32[6,4,512]{2,1,0:T(4,128)S(1)} %get-tuple-element.18), channel_id=1, source_target_pairs={{0,1},{1,0},{2,3},{3,2},{4,5},{5,4},{6,7},{7,6},{8,9},{9,8},{10,11... | collective-permute-start | bytes 147464 | tf_op jit(solution)/shard_map/ppermute | solution.py:173
  334.8 46.8 %all-to-all-start.1 = ((bf16[128,2,8,768]{3,2,1,0:T(8,128)(2,1)}), bf16[128,2,8,768]{3,2,1,0:T(8,128)(2,1)S(1)}, u32[]{:S(2)}, u32[]{:S(2)}) async-start(bf16[128,2,8,768]{3,2,1,0:T(8,128)(2,1)} %bitcast.35), calls=%async_computation.1 | async-start | bytes 6291456 | tf_op jit(solution)/shard_map/all_to_all | solution.py:232
  381.6 47.1 %copy-start = (bf16[128,2,8,768]{3,2,1,0:T(8,128)(2,1)}, bf16[128,2,8,768]{3,2,1,0:T(8,128)(2,1)S(1)}, u32[]{:S(2)}) copy-start(bf16[128,2,8,768]{3,2,1,0:T(8,128)(2,1)S(1)} %all-to-all-done.1.in0_ref) | copy-start | bytes 9437188
Sparse Core Ops, SparseCore 0:
  12.2 213.8 all-gather.6
  229.2 67.0 all-gather.4

commit v2 on v0

v2 whole, which is shorter than its diff:
```python
import jax
import jax.numpy as jnp
import numpy as np
from jax import lax
from jax.experimental import pallas as pl
from jax.experimental.pallas import tpu as pltpu
from jax.sharding import PartitionSpec as P


BLK = 128
HALF = 768
BW = 384
WIDE = 1536
VMEM = 56 * 1024 * 1024
BOTH = ("ctx", "ch")
N_CTX = 64


def z_hi(i):
    return (i // 8) % 2


SIDES = [[2 * i + (s ^ z_hi(i)) for i in range(N_CTX)] for s in range(2)]
PLANES = [[i for i in range(N_CTX) if z_hi(i) == z and i % 2 == core] for z in range(2) for core in range(2)]


def limits(exponent):
    return lax.shift_left(jnp.ones_like(exponent), exponent + 9).astype(jnp.float32) * 0.875


def regroup_matrix():
    matrix = np.zeros((256, 256), np.float32)
    for i in range(16):
        for r in range(2):
            for a in range(8):
                matrix[i * 16 + r * 8 + a, a * 32 + i * 2 + r] = 1.0
    return matrix


def first_kernel(mix_ref, perm_ref, tok_ref, spec_ref, exp_ref, out_ref, enc_ref):
    columns = limits(exp_ref[0]).T
    mix = mix_ref[...]
    for pair in range(4):
        rhs = jnp.concatenate([tok_ref[2 * pair], tok_ref[2 * pair + 1]], axis=1)
        acc = jnp.dot(mix, rhs, preferred_element_type=jnp.float32)
        for side in range(2):
            a = 2 * pair + side
            value = acc[:, side * BLK:(side + 1) * BLK] * spec_ref[a].astype(jnp.float32)
            top = columns[:, a:a + 1]
            enc_ref[a] = jnp.clip(value, -top, top).astype(jnp.bfloat16)
    for g in range(4):
        for h in range(2):
            both = jnp.concatenate(
                [
                    enc_ref[:, s * 256 + h * 128 + g * 32:s * 256 + h * 128 + (g + 1) * 32, :].reshape(256, BLK)
                    for s in range(2)
                ],
                axis=1,
            )
            moved = jnp.dot(perm_ref[...], both, preferred_element_type=jnp.float32).astype(jnp.bfloat16)
            for s in range(2):
                cols = slice(s * BLK, (s + 1) * BLK)
                out_ref[g * 16:g * 16 + 8, s, h] = moved[:128, cols].reshape(8, 16, BLK)
                out_ref[g * 16 + 8:g * 16 + 16, 1 - s, h] = moved[128:, cols].reshape(8, 16, BLK)


def first_stage(mix_first, perm, tokens, spectral, exponents):
    wide = pl.BlockSpec((8, 512, BLK), lambda d: (0, 0, d))
    return pl.pallas_call(
        first_kernel,
        grid=(HALF // BLK,),
        in_specs=[
            pl.BlockSpec((512, 512), lambda d: (0, 0)),
            pl.BlockSpec((256, 256), lambda d: (0, 0)),
            wide,
            wide,
            pl.BlockSpec((1, 8, 512), lambda d: (d, 0, 0)),
        ],
        out_specs=pl.BlockSpec((N_CTX, 2, 2, 16, BLK), lambda d: (0, 0, 0, 0, d)),
        out_shape=jax.ShapeDtypeStruct((N_CTX, 2, 2, 16, HALF), jnp.bfloat16),
        scratch_shapes=[pltpu.VMEM((8, 512, BLK), jnp.bfloat16)],
        compiler_params=pltpu.CompilerParams(vmem_limit_bytes=VMEM),
        cost_estimate=pl.CostEstimate(flops=4_800_000_000, bytes_accessed=18_900_000, transcendentals=0),
        name="first_mix",
    )(mix_first, perm, tokens, spectral, exponents)


def second_kernel(mix_ref, recv_ref, exp_ref, out_ref):
    columns = limits(exp_ref[0, 0]).T
    right = recv_ref[:, 0, 0].reshape(1024, 256)
    for m in range(4):
        rows = slice(m * 256, (m + 1) * 256)
        acc = jnp.dot(mix_ref[rows, :], right, preferred_element_type=jnp.float32)
        for n in range(2):
            top = columns[rows, n:n + 1]
            held = jnp.clip(acc[:, n * BLK:(n + 1) * BLK], -top, top).astype(jnp.bfloat16)
            out_ref[m * 16:(m + 1) * 16, :, n * BLK:(n + 1) * BLK] = held.reshape(16, 16, BLK)


def second_stage(mix, received, exponents, h):
    return pl.pallas_call(
        second_kernel,
        grid=(6,),
        in_specs=[
            pl.BlockSpec((1024, 1024), lambda n: (0, 0)),
            pl.BlockSpec((N_CTX, 1, 1, 16, 256), lambda n: (0, n // 3, h, 0, n % 3)),
            pl.BlockSpec((1, 1, 2, 1024), lambda n: (h, n, 0, 0)),
        ],
        out_specs=pl.BlockSpec((N_CTX, 16, 256), lambda n: (0, 0, n)),
        out_shape=jax.ShapeDtypeStruct((N_CTX, 16, WIDE), jnp.bfloat16),
        compiler_params=pltpu.CompilerParams(vmem_limit_bytes=VMEM),
        cost_estimate=pl.CostEstimate(flops=3_200_000_000, bytes_accessed=8_400_000, transcendentals=0),
        name="second_mix",
    )(mix, received, exponents)


def peel_kernel(place_ref, tok_ref, after_ref, out0_ref, out1_ref):
    del place_ref, after_ref
    out0_ref[...] = tok_ref[:, :128, :]
    out1_ref[...] = tok_ref[:, 128:, :]


def peel_stage(place, tokens, after):
    out = jax.ShapeDtypeStruct((8, 128, HALF), jnp.bfloat16)
    out_spec = pl.BlockSpec((8, 128, 256), lambda d, place: (0, 0, d))
    return pl.pallas_call(
        peel_kernel,
        grid_spec=pltpu.PrefetchScalarGridSpec(
            num_scalar_prefetch=1,
            grid=(3,),
            in_specs=[
                pl.BlockSpec((8, 256, 256), lambda d, place: (0, 1 - place[0], d)),
                pl.BlockSpec(memory_space=pl.ANY),
            ],
            out_specs=[out_spec, out_spec],
        ),
        out_shape=[out, out],
        compiler_params=pltpu.CompilerParams(vmem_limit_bytes=VMEM),
        cost_estimate=pl.CostEstimate(flops=0, bytes_accessed=6_300_000, transcendentals=0),
        name="tokens_to_send",
    )(place, tokens, after)


def mixer_kernel(
    place_ref, perm_ref, recv_ref, own_tok_ref, far_tok_ref, own_gate_ref, far_gate_ref,
    own_up_ref, far_up_ref, own_down_ref, far_down_ref, *rest
):
    own_out_ref, far_out_ref, gated_ref = rest[-3:]
    c = place_ref[1]
    toks = (own_tok_ref, far_tok_ref)
    gates = (own_gate_ref, far_gate_ref)
    ups = (own_up_ref, far_up_ref)
    downs = (own_down_ref, far_down_ref)
    starts = (pl.multiple_of(c * HALF, BLK), pl.multiple_of((1 - c) * HALF, BLK))
    for p in range(2):
        mixed = jnp.dot(
            perm_ref[...],
            recv_ref[:, :, pl.ds(starts[p], HALF)].reshape(256, HALF),
            preferred_element_type=jnp.float32,
        )
        tok = toks[p][...].reshape(256, HALF).astype(jnp.float32)
        slope = jax.nn.sigmoid(tok * gates[p][...])
        gated_ref[p] = (tok + mixed * slope).astype(jnp.bfloat16)
    for q in range(2):
        totals = [None, None]
        for p in range(2):
            hidden = []
            for i in range(2):
                pre = jnp.dot(
                    gated_ref[p, :, i * BW:(i + 1) * BW],
                    ups[p][i, :, pl.ds(starts[q], HALF)],
                    preferred_element_type=jnp.float32,
                )
                hidden.append(jax.nn.gelu(pre, approximate=True).astype(jnp.bfloat16))
            for k in range(2):
                left = jnp.concatenate([part[:, k * BW:(k + 1) * BW] for part in hidden], axis=1)
                right = downs[p][:, :, pl.ds(pl.multiple_of(starts[q] + k * BW, BLK), BW)].reshape(HALF, BW)
                part = jnp.dot(left, right, preferred_element_type=jnp.float32)
                totals[k] = part if p == 0 else totals[k] + part
        out_ref = (own_out_ref, far_out_ref)[q]
        for k in range(2):
            cols = slice(k * BW, (k + 1) * BW)
            result = gated_ref[q, :, cols].astype(jnp.float32) + totals[k]
            out_ref[:, :, cols] = result.astype(jnp.bfloat16).reshape(8, 32, BW)


def mixer_stage(place, perm, received, tokens, far_tokens, gates, ups, downs, whole, h, u):
    weight = pl.BlockSpec((2, BW, WIDE), lambda p, place: (0, 0, 0))
    gate = pl.BlockSpec((1, HALF), lambda p, place: (0, 0))
    own = pl.BlockSpec((8, 32, HALF), lambda p, place: (0, 8 * place[0] + 4 * h + 2 * u + p, 0))
    in_specs = [
        pl.BlockSpec((256, 256), lambda p, place: (0, 0)),
        pl.BlockSpec((16, 16, WIDE), lambda p, place: (2 * u + p, 0, 0)),
        own,
        pl.BlockSpec((8, 32, HALF), lambda p, place: (0, 2 * u + p, 0)),
        gate, gate, weight, weight, weight, weight,
    ]
    operands = [perm, received, tokens, far_tokens, *gates, *ups, *downs]
    aliases = {}
    if whole is not None:
        aliases = {len(operands) + 1: 0}
        in_specs.append(pl.BlockSpec(memory_space=pl.ANY))
        operands.append(whole)
    return pl.pallas_call(
        mixer_kernel,
        grid_spec=pltpu.PrefetchScalarGridSpec(
            num_scalar_prefetch=1,
            grid=(2,),
            in_specs=in_specs,
            out_specs=[own, pl.BlockSpec((8, 32, HALF), lambda p, place: (0, p, 0))],
            scratch_shapes=[pltpu.VMEM((2, 256, HALF), jnp.bfloat16)],
        ),
        out_shape=[
            jax.ShapeDtypeStruct((8, 512, HALF), jnp.bfloat16),
            jax.ShapeDtypeStruct((8, 64, HALF), jnp.bfloat16),
        ],
        input_output_aliases=aliases,
        compiler_params=pltpu.CompilerParams(vmem_limit_bytes=VMEM),
        cost_estimate=pl.CostEstimate(
            flops=6_000_000_000, bytes_accessed=14_000_000, transcendentals=4_000_000
        ),
        name="channel_mix",
    )(place, *operands)


def swap(value):
    return lax.ppermute(value, "ch", [(0, 1), (1, 0)])


def swap_cores(value):
    return lax.ppermute(value, "ctx", [(i, i ^ 1) for i in range(N_CTX)])


def exponent_route(step):
    pairs = []
    for i0 in range(N_CTX):
        for c0 in range(2):
            s, h = i0 // 32, (i0 // 16) % 2
            i = 4 * (i0 % 16) + ((2 * h + c0) ^ step)
            pairs.append((2 * i0 + c0, 2 * i + (s ^ z_hi(i))))
    return pairs


def routed_exponents(second_exponents, ctx, ch):
    columns = second_exponents.transpose(2, 1, 0)
    source = 2 * ((ctx // 16) % 2) + ch
    got = []
    for step in range(4):
        rows = lax.dynamic_slice_in_dim(columns, 2 * (source ^ step), 2, 1)
        got.append(lax.ppermute(rows, BOTH, exponent_route(step)))

    def finish():
        stacked = jnp.stack(got)
        ordered = jnp.stack(
            [lax.dynamic_index_in_dim(stacked, v ^ (ctx % 4), 0, keepdims=False) for v in range(4)]
        )
        split = ordered.reshape(2, 2, 6, 2, N_CTX, 8)
        return split.transpose(0, 1, 2, 4, 3, 5).reshape(2, 6, 2, 1024)

    return got, finish


def doubled_mix(mix):
    row = lax.broadcasted_iota(jnp.int32, (1024, 512), 0)
    col = lax.broadcasted_iota(jnp.int32, (1024, 512), 1)
    pick = ((row // 16) * 8 + row % 8 == col).astype(jnp.bfloat16)
    tall = jnp.dot(pick, mix, preferred_element_type=jnp.float32).astype(jnp.bfloat16)
    full = lax.dot_general(tall, pick, (((1,), (1,)), ((), ())), preferred_element_type=jnp.float32)
    row = lax.broadcasted_iota(jnp.int32, (1024, 1024), 0)
    col = lax.broadcasted_iota(jnp.int32, (1024, 1024), 1)
    return jnp.where((row // 8) % 2 == (col // 8) % 2, full, 0.0).astype(jnp.bfloat16)


def body(
    tokens,
    mix_first,
    mix_second,
    spectral_kernel,
    gate_scale,
    up_weight,
    down_weight,
    first_exponents,
    second_exponents,
):
    ctx = lax.axis_index("ctx")
    ch = lax.axis_index("ch")
    core = ctx % 2
    side = ch ^ ((ctx // 8) % 2)
    place = jnp.stack([side, ch]).astype(jnp.int32)
    perm = regroup_matrix()

    rows = 2 * BW
    piece = rows // 16
    start = ((ctx // 16) * 4 + (ctx % 8) // 2) * piece
    cut = lambda w: lax.dynamic_slice_in_dim(w.reshape(rows, 4, BW), start, piece, 0).reshape(piece, WIDE)
    slice_far = swap(jnp.where(core == 0, cut(up_weight), cut(down_weight)))
    own_gate = gate_scale.reshape(1, HALF)
    far_gate = swap(own_gate)
    exps, finish_exps = routed_exponents(second_exponents, ctx, ch)

    send = first_stage(
        mix_first,
        jnp.asarray(perm, jnp.bfloat16),
        tokens,
        spectral_kernel,
        first_exponents.transpose(2, 0, 1),
    )
    send, slice_far, far_gate, exps[:] = lax.optimization_barrier((send, slice_far, far_gate, list(exps)))
    gathered = lax.all_gather(slice_far, "ctx", axis=0, tiled=True, axis_index_groups=PLANES)
    received = lax.all_to_all(
        send.reshape(128, 2, 16, HALF), BOTH, split_axis=0, concat_axis=0, tiled=True
    ).reshape(N_CTX, 2, 2, 16, HALF)

    crossed = swap_cores(gathered)
    whole_shape = (2, BW, WIDE)
    far_up = jnp.where(core == 0, gathered, crossed).reshape(whole_shape)
    far_down = jnp.where(core == 0, crossed, gathered).reshape(whole_shape)
    ups = (up_weight.reshape(whole_shape), far_up)
    downs = (down_weight.reshape(whole_shape), far_down)
    gates = (own_gate, far_gate)
    mix = doubled_mix(mix_second)
    tops = finish_exps()

    far_tokens = [swap(part) for part in peel_stage(place, tokens, received)]
    whole = None
    back = []
    perm_back = jnp.asarray(perm.T, jnp.bfloat16)
    for h in range(2):
        second = second_stage(mix, received, tops, h)
        mixed = lax.all_to_all(
            second, BOTH, split_axis=0, concat_axis=0, tiled=True, axis_index_groups=SIDES
        )
        for u in range(2):
            whole, far = mixer_stage(
                place, perm_back, mixed, tokens, far_tokens[h], gates, ups, downs, whole, h, u
            )
            back.append(swap(far))
    for n, part in enumerate(back):
        whole = lax.dynamic_update_slice_in_dim(whole, part, (1 - side) * 256 + 64 * n, 1)
    return whole


def solution(mesh):
    placed = (
        P("ctx", None, "ch"),
        P(),
        P(),
        P("ctx", None, "ch"),
        P("ch"),
        P("ch", None, None, None),
        P("ch", None, None, None),
        P("ctx", None, "ch"),
        P(None, "ctx", "ch"),
    )
    return jax.shard_map(
        body, mesh=mesh, in_specs=placed, out_specs=P("ctx", None, "ch"), check_vma=False
    )
```

time: 753 us -> 354 us (0.47)
  waiting for transfers between devices: 410 us -> 156 us
  local copies, waits for them, and re-layouts: 165 us -> 23.7 us
  Pallas kernels: 0 us -> 92.9 us
  other arithmetic: 58.8 us -> 6.61 us
  matrix products: 55.6 us -> 5.17 us
  starting transfers between devices: 41.8 us -> 54.2 us
    psum x1 -> x0, waiting for transfers between devices: 294 us -> none  [body(): lax.psum(partial_value.astype(jnp.bfloat16), 'ch').astype(jnp.float32)]
    pallas_call x0 -> x8, Pallas kernels: none -> 92.9 us  [the longest x4 58 us: mixer_stage(): pl.pallas_call(mixer_kernel, grid_spec=pltpu.PrefetchScalarGridSpec(num_s...]
    reshape x4 -> x5, local copies, waits for them, and re-layouts: 92.6 us -> 13.4 us  [the longest x1 5.03 us: body(): downs = (down_weight.reshape(whole_shape), far_down)]
    convert_element_type x8 -> x0, other arithmetic: 57.5 us -> none  [the longest x1 13 us: body(): gated_seq = (plain_tok + mixed_seq.astype(jnp.float32) * jax.nn.sigmoid(p...]
    ppermute x0 -> x13, waiting for transfers between devices: none -> 57.1 us  [the longest x8 57.1 us: swap(): return lax.ppermute(value, 'ch', [(0, 1), (1, 0)])]
    dot_general x3 -> x2, matrix products: 55.6 us -> 5.17 us  [the longest x1 3.17 us: doubled_mix(): lax.dot_general(tall, pick, (((1,), (1,)), ((), ())), preferred_element_t...]
    convert_element_type x9 -> x0, local copies, waits for them, and re-layouts: 35.5 us -> none  [the longest x5 13.9 us: decode_blocks(): scales.astype(jnp.float32)]
    ppermute x0 -> x13, starting transfers between devices: none -> 26.2 us  [the longest x4 18.8 us: routed_exponents(): got.append(lax.ppermute(rows, BOTH, exponent_route(step)))]
  transfers between devices with their start and end apart: 5 -> 17, of which waited for: 3 -> 7; matrix products, arithmetic and copies ran while one was open for 17% -> 9% of each run, Pallas kernels for 0% -> 26%
where the time goes in v2:
time: 354 us; the launch traced here: 353 us
  waiting for transfers between devices  156 us (44%)
  Pallas kernels  92.9 us (26%)
  starting transfers between devices  54.2 us (15%)
  local copies, waits for them, and re-layouts  23.7 us (7%)
  between operations  13.7 us (4%)
  other arithmetic  6.61 us (2%)
  matrix products  5.17 us (1%)
    all_to_all x1, waiting for transfers between devices, body(): lax.all_to_all(send.reshape(128, 2, 16, HALF), BOTH, split_axis=0, concat...  66.4 us
    pallas_call x4, Pallas kernels, mixer_stage(): pl.pallas_call(mixer_kernel, grid_spec=pltpu.PrefetchScalarGridSpec(num_s...  58 us
    ppermute x8, waiting for transfers between devices, swap(): return lax.ppermute(value, 'ch', [(0, 1), (1, 0)])  57.1 us
    all_to_all x2, waiting for transfers between devices, body(): lax.all_to_all(second, BOTH, split_axis=0, concat_axis=0, tiled=True, axi...  32.2 us
    ppermute x4, starting transfers between devices, routed_exponents(): got.append(lax.ppermute(rows, BOTH, exponent_route(step)))  18.8 us
    pallas_call x2, Pallas kernels, second_stage(): pl.pallas_call(second_kernel, grid=(6,), in_specs=[pl.BlockSpec((1024, 10...  17.2 us
    all_to_all x2, starting transfers between devices, body(): lax.all_to_all(second, BOTH, split_axis=0, concat_axis=0, tiled=True, axi...  16.8 us
    pallas_call x1, Pallas kernels, first_stage(): pl.pallas_call(first_kernel, grid=(HALF // BLK,), in_specs=[pl.BlockSpec(...  12.4 us
  transfers between devices with their start and end apart: 17, of which 7 were waited for; matrix products, arithmetic and copies ran while one was open for 9% of the time, Pallas kernels for 26%

profile of v2, /device:TPU:1, one launch (start us, length us, event | category | flops | bytes accessed | tf_op | source)
XLA Modules:
  0.0 352.7 jit_solution(6463610172391535013)
XLA Ops:
  6.5 0.0 copy-start
  6.5 1.1 dynamic-slice_select_fusion
  7.7 2.5 collective-permute-start
  10.2 0.7 reshape.39.own_gate_ref
  10.9 0.0 collective-permute-start.1
  10.9 1.1 dynamic-slice_bitcast_fusion
  12.1 5.8 %collective-permute-start.2 = (s32[6,2,512]{2,1,0:T(2,128)S(1)}, s32[6,2,512]{2,1,0:T(2,128)S(1)}, u32[]{:S(2)}, u32[]{:S(2)}) collective-permute-start(s32[6,2,512]{2,1,0:T(2,128)S(1)} %get-tuple-element.47), channel_id=1, source_target_pairs={{0,0},{1,2},{2,8},{3,10},{4,17},{5,19},{6,25},{7,27},{8,32},{9,34}... | collective-permute-start | bytes 73736 | tf_op jit(solution)/shard_map/ppermute | solution.py:250
  17.8 3.1 collective-permute-start.3
  21.0 6.5 %collective-permute-start.4 = (s32[6,2,512]{2,1,0:T(2,128)S(1)}, s32[6,2,512]{2,1,0:T(2,128)S(1)}, u32[]{:S(2)}, u32[]{:S(2)}) collective-permute-start(s32[6,2,512]{2,1,0:T(2,128)S(1)} %get-tuple-element.48), channel_id=1, source_target_pairs={{0,4},{1,6},{2,12},{3,14},{4,21},{5,23},{6,29},{7,31},{8,36},{9,38... | collective-permute-start | bytes 73736 | tf_op jit(solution)/shard_map/ppermute | solution.py:250
  27.5 0.0 collective-permute-done.1.far_gate_ref
  27.5 0.0 copy-start.6
  27.5 3.4 collective-permute-start.5
  30.9 12.4 %first_mix.1 = bf16[64,2,2,16,768]{4,3,2,1,0:T(8,128)(2,1)} custom-call(bf16[512,512]{1,0:T(8,128)(2,1)} %mix_ref.1, bf16[256,256]{1,0:T(8,128)(2,1)} %constant.185.clone.perm_ref, bf16[8,512,768]{2,1,0:T(8,128)(2,1)} %own_tok_ref.7, bf16[8,512,768]{2,1,0:T(8,128)(2,1)} %spec_ref.1, s32[6,8,512]{2,1,0:T(8,128)} %bitcast.44), custom_call_target="tpu_custom_call" | custom-call | flops 4800000000 | bytes 18900000 | tf_op jit(solution)/shard_map/first_mix/pallas_call | solution.py:69
  43.3 0.0 copy-done.6
  43.3 0.0 collective-permute-done.2
  43.3 0.0 collective-permute-done.3
  43.3 0.0 collective-permute-done.4
  43.3 0.0 collective-permute-done.5
  43.3 0.0 collective-permute-done
  43.3 0.6 copy-done.4
  44.0 11.1 %all-to-all-start = ((bf16[128,2,16,768]{3,2,1,0:T(8,128)(2,1)}), bf16[128,2,16,768]{3,2,1,0:T(8,128)(2,1)}, u32[]{:S(2)}, u32[]{:S(2)}) async-start(bf16[128,2,16,768]{3,2,1,0:T(8,128)(2,1)} %bitcast.38), calls=%async_computation | async-start | bytes 12582912 | tf_op jit(solution)/shard_map/all_to_all | solution.py:310
  55.1 0.0 all-gather.2.cloned.1.call-start
  55.2 0.7 all-gather.2.cloned.1.call-update
  56.0 2.0 convolution_convert_fusion.clone.5
  58.0 3.2 select_convert_fusion.mix_ref
  61.2 0.9 reshape.42
  62.1 2.4 copy.16
  64.5 4.4 %reshape.43.exp_ref = s32[2,6,2,1024]{3,2,1,0:T(2,128)} reshape(s32[2,2,6,64,2,8]{5,4,3,2,1,0:T(2,128)} %copy.16) | data formatting | bytes 196608 | tf_op jit(solution)/shard_map/reshape | solution.py:258
  68.9 66.4 %all-to-all-done = bf16[128,2,16,768]{3,2,1,0:T(8,128)(2,1)} async-done(((bf16[128,2,16,768]{3,2,1,0:T(8,128)(2,1)}), bf16[128,2,16,768]{3,2,1,0:T(8,128)(2,1)}, u32[]{:S(2)}, u32[]{:S(2)}) %all-to-all-start) | async-done | bytes 6291488 | tf_op jit(solution)/shard_map/all_to_all | solution.py:310
  135.3 8.6 %second_mix.3 = bf16[64,16,1536]{2,1,0:T(8,128)(2,1)} custom-call(bf16[1024,1024]{1,0:T(8,128)(2,1)} %select_convert_fusion.mix_ref, bf16[64,2,2,16,768]{4,3,2,1,0:T(8,128)(2,1)} %bitcast.10.recv_ref.after_ref, s32[2,6,2,1024]{3,2,1,0:T(2,128)} %reshape.43.exp_ref), custom_call_target="tpu_custom_call" | custom-call | flops 3200000000 | bytes 8400000 | tf_op jit(solution)/shard_map/second_mix/pallas_call | solution.py:101
  143.9 11.1 %all-to-all-start.2 = ((bf16[64,16,1536]{2,1,0:T(8,128)(2,1)}), bf16[64,16,1536]{2,1,0:T(8,128)(2,1)}, u32[]{:S(2)}, u32[]{:S(2)}) async-start(bf16[64,16,1536]{2,1,0:T(8,128)(2,1)} %second_mix.3), calls=%async_computation.2 | async-start | bytes 6291456 | tf_op jit(solution)/shard_map/all_to_all | solution.py:330
  155.0 0.0 all-gather.2.cloned.1.call-done
  155.1 0.6 collective-permute-start.7
  155.7 8.6 %second_mix.2 = bf16[64,16,1536]{2,1,0:T(8,128)(2,1)} custom-call(bf16[1024,1024]{1,0:T(8,128)(2,1)} %select_convert_fusion.mix_ref, bf16[64,2,2,16,768]{4,3,2,1,0:T(8,128)(2,1)} %bitcast.10.recv_ref.after_ref, s32[2,6,2,1024]{3,2,1,0:T(2,128)} %reshape.43.exp_ref), custom_call_target="tpu_custom_call" | custom-call | flops 3200000000 | bytes 8400000 | tf_op jit(solution)/shard_map/second_mix/pallas_call | solution.py:101
  164.3 32.2 %all-to-all-done.2.recv_ref = bf16[64,16,1536]{2,1,0:T(8,128)(2,1)} async-done(((bf16[64,16,1536]{2,1,0:T(8,128)(2,1)}), bf16[64,16,1536]{2,1,0:T(8,128)(2,1)}, u32[]{:S(2)}, u32[]{:S(2)}) %all-to-all-start.2) | async-done | bytes 3145760 | tf_op jit(solution)/shard_map/all_to_all | solution.py:330
  196.5 5.7 %all-to-all-start.1 = ((bf16[64,16,1536]{2,1,0:T(8,128)(2,1)}), bf16[64,16,1536]{2,1,0:T(8,128)(2,1)}, u32[]{:S(2)}, u32[]{:S(2)}) async-start(bf16[64,16,1536]{2,1,0:T(8,128)(2,1)} %second_mix.2), calls=%async_computation.1 | async-start | bytes 6291456 | tf_op jit(solution)/shard_map/all_to_all | solution.py:330
  202.2 0.6 pad_add_fusion.2.place_ref
  202.8 5.4 %tokens_to_send.1 = (bf16[8,128,768]{2,1,0:T(8,128)(2,1)}, bf16[8,128,768]{2,1,0:T(8,128)(2,1)}) custom-call(s32[2]{0:T(128)} %pad_add_fusion.2.place_ref, bf16[8,512,768]{2,1,0:T(8,128)(2,1)} %own_tok_ref.7, bf16[64,2,2,16,768]{4,3,2,1,0:T(8,128)(2,1)} %bitcast.10.recv_ref.after_ref), custom_call_target="tpu_custom_call" | custom-call | bytes 6300000 | tf_op jit(solution)/shard_map/tokens_to_send/pallas_call | solution.py:126
  208.2 0.1 collective-permute-start.8
  208.3 2.3 reshape.44.own_up_ref
  210.7 5.0 %reshape.46.own_down_ref = bf16[2,384,1536]{2,1,0:T(8,128)(2,1)} reshape(bf16[2,384,4,384]{3,2,1,0:T(4,128)(2,1)} %param.17) | data formatting | bytes 4718592 | tf_op jit(solution)/shard_map/reshape | solution.py:319
  215.7 1.3 collective-permute-start.6
  217.0 0.0 collective-permute-done.7
  217.0 4.9 %broadcast_select_fusion = (bf16[768,1536]{1,0:T(8,128)(2,1)}, bf16[768,1536]{1,0:T(8,128)(2,1)}) fusion(bf16[768,1536]{1,0:T(8,128)(2,1)} %collective-permute-done.7, bf16[768,1536]{1,0:T(8,128)(2,1)} %all-gather.2.cloned.1.call-done, pred[]{:T(512)S(6)} %eq.29), kind=kLoop, calls=%fused_computation.14 | loop fusion | flops 2359296 | bytes 9437185 | tf_op jit(solution)/shard_map/jit(_where)/select_n | solution.py:317
  221.9 22.1 %collective-permute-done.8.far_tok_ref = bf16[8,128,768]{2,1,0:T(8,128)(2,1)} collective-permute-done((bf16[8,128,768]{2,1,0:T(8,128)(2,1)}, bf16[8,128,768]{2,1,0:T(8,128)(2,1)}, u32[]{:S(2)}, u32[]{:S(2)}) %collective-permute-start.8) | collective-permute-done | bytes 1572896 | tf_op jit(solution)/shard_map/ppermute | solution.py:227
  243.9 14.5 %channel_mix.4 = (bf16[8,512,768]{2,1,0:T(8,128)(2,1)}, bf16[8,64,768]{2,1,0:T(8,128)(2,1)}) custom-call(s32[2]{0:T(128)} %pad_add_fusion.2.place_ref, bf16[256,256]{1,0:T(8,128)(2,1)} %constant.186.clone.perm_ref, bf16[64,16,1536]{2,1,0:T(8,128)(2,1)} %all-to-all-done.2.recv_ref, bf16[8,512,768]{2,1,0:T(8,128)(2,1)} %own_tok_ref.7, ...), custom_call_target="tpu_custom_call" | custom-call | flops 6000000000 | bytes 14000000 | tf_op jit(solution)/shard_map/channel_mix/pallas_call | solution.py:204
  258.4 0.1 collective-permute-start.9
  258.5 14.5 %channel_mix.5 = (bf16[8,512,768]{2,1,0:T(8,128)(2,1)}, bf16[8,64,768]{2,1,0:T(8,128)(2,1)}) custom-call(s32[2]{0:T(128)} %pad_add_fusion.2.place_ref, bf16[256,256]{1,0:T(8,128)(2,1)} %constant.186.clone.perm_ref, bf16[64,16,1536]{2,1,0:T(8,128)(2,1)} %all-to-all-done.2.recv_ref, ...), custom_call_target="tpu_custom_call", output_to_operand_aliasing={{0}: (11, {})} | custom-call | flops 6000000000 | bytes 14000000 | tf_op jit(solution)/shard_map/channel_mix/pallas_call | solution.py:204
  273.0 1.3 collective-permute-start.10
  274.4 3.2 collective-permute-done.6.far_tok_ref
  277.5 0.0 all-to-all-done.1.recv_ref
  277.5 1.2 copy-done.2
  278.7 14.5 %channel_mix.6 = (bf16[8,512,768]{2,1,0:T(8,128)(2,1)}, bf16[8,64,768]{2,1,0:T(8,128)(2,1)}) custom-call(s32[2]{0:T(128)} %pad_add_fusion.2.place_ref, bf16[256,256]{1,0:T(8,128)(2,1)} %constant.186.clone.perm_ref, bf16[64,16,1536]{2,1,0:T(8,128)(2,1)} %all-to-all-done.1.recv_ref, ...), custom_call_target="tpu_custom_call", output_to_operand_aliasing={{0}: (11, {})} | custom-call | flops 6000000000 | bytes 14000000 | tf_op jit(solution)/shard_map/channel_mix/pallas_call | solution.py:204
  293.2 0.1 collective-permute-start.11
  293.3 14.5 %channel_mix.7 = (bf16[8,512,768]{2,1,0:T(8,128)(2,1)}, bf16[8,64,768]{2,1,0:T(8,128)(2,1)}) custom-call(s32[2]{0:T(128)} %pad_add_fusion.2.place_ref, bf16[256,256]{1,0:T(8,128)(2,1)} %constant.186.clone.perm_ref, bf16[64,16,1536]{2,1,0:T(8,128)(2,1)} %all-to-all-done.1.recv_ref, ...), custom_call_target="tpu_custom_call", output_to_operand_aliasing={{0}: (11, {})} | custom-call | flops 6000000000 | bytes 14000000 | tf_op jit(solution)/shard_map/channel_mix/pallas_call | solution.py:204
  307.8 1.3 collective-permute-start.12
  309.1 0.0 collective-permute-done.9
  309.1 0.9 constant_dynamic-update-slice_fusion.3
  310.1 1.3 collective-permute-done.10
  311.3 2.1 constant_dynamic-update-slice_fusion.2
  313.4 14.7 %collective-permute-done.11 = bf16[8,64,768]{2,1,0:T(8,128)(2,1)S(1)} collective-permute-done((bf16[8,64,768]{2,1,0:T(8,128)(2,1)}, bf16[8,64,768]{2,1,0:T(8,128)(2,1)S(1)}, u32[]{:S(2)}, u32[]{:S(2)}) %collective-permute-start.11) | collective-permute-done | bytes 786464 | tf_op jit(solution)/shard_map/ppermute | solution.py:227
  328.1 0.9 constant_dynamic-update-slice_fusion.1
  329.0 15.9 %collective-permute-done.12 = bf16[8,64,768]{2,1,0:T(8,128)(2,1)S(1)} collective-permute-done((bf16[8,64,768]{2,1,0:T(8,128)(2,1)}, bf16[8,64,768]{2,1,0:T(8,128)(2,1)S(1)}, u32[]{:S(2)}, u32[]{:S(2)}) %collective-permute-start.12) | collective-permute-done | bytes 786464 | tf_op jit(solution)/shard_map/ppermute | solution.py:227
  344.9 0.9 constant_dynamic-update-slice_fusion
  (18 shorter events, 0.1 us)
Async XLA Ops:
  6.5 49.4 %copy-start = (bf16[512,512]{1,0:T(8,128)(2,1)S(1)}, bf16[512,512]{1,0:T(8,128)(2,1)}, u32[]{:S(2)}) copy-start(bf16[512,512]{1,0:T(8,128)(2,1)} %param.13) | copy-start | bytes 1572868
  7.7 35.6 %collective-permute-start = (bf16[48,1536]{1,0:T(8,128)(2,1)S(1)}, bf16[48,1536]{1,0:T(8,128)(2,1)S(1)}, u32[]{:S(2)}, u32[]{:S(2)}) collective-permute-start(bf16[48,1536]{1,0:T(8,128)(2,1)S(1)} %bitcast.43), channel_id=1, source_target_pairs={{0,1},{1,0},{2,3},{3,2},{4,5},{5,4},{6,7},{7,6},{8,9},{9,8},{10,11... | collective-permute-start | bytes 442376 | tf_op jit(solution)/shard_map/ppermute | solution.py:227
  10.9 32.3 %copy-start.5 = (f32[1,768]{1,0:T(1,128)}, f32[1,768]{1,0:T(1,128)S(1)}, u32[]{:S(2)}) copy-start(f32[1,768]{1,0:T(1,128)S(1)} %reshape.39.own_gate_ref) | copy-start | bytes 9220
  10.9 16.5 %collective-permute-start.1 = (f32[1,768]{1,0:T(1,128)S(1)}, f32[1,768]{1,0:T(1,128)S(1)}, u32[]{:S(2)}, u32[]{:S(2)}) collective-permute-start(f32[1,768]{1,0:T(1,128)S(1)} %reshape.39.own_gate_ref), channel_id=1, source_target_pairs={{0,1},{1,0},{2,3},{3,2},{4,5},{5,4},{6,7},{7,6},{8,9},{9,8},{10,11... | collective-permute-start | bytes 9224 | tf_op jit(solution)/shard_map/ppermute | solution.py:227
  12.1 31.2 %collective-permute-start.2 = (s32[6,2,512]{2,1,0:T(2,128)S(1)}, s32[6,2,512]{2,1,0:T(2,128)S(1)}, u32[]{:S(2)}, u32[]{:S(2)}) collective-permute-start(s32[6,2,512]{2,1,0:T(2,128)S(1)} %get-tuple-element.47), channel_id=1, source_target_pairs={{0,0},{1,2},{2,8},{3,10},{4,17},{5,19},{6,25},{7,27},{8,32},{9,34}... | collective-permute-start | bytes 73736 | tf_op jit(solution)/shard_map/ppermute | solution.py:250
  17.8 25.5 %collective-permute-start.3 = (s32[6,2,512]{2,1,0:T(2,128)S(1)}, s32[6,2,512]{2,1,0:T(2,128)S(1)}, u32[]{:S(2)}, u32[]{:S(2)}) collective-permute-start(s32[6,2,512]{2,1,0:T(2,128)S(1)} %get-tuple-element.46), channel_id=1, source_target_pairs={{0,2},{1,0},{2,10},{3,8},{4,19},{5,17},{6,27},{7,25},{8,34},{9,32}... | collective-permute-start | bytes 73736 | tf_op jit(solution)/shard_map/ppermute | solution.py:250
  21.0 22.3 %collective-permute-start.4 = (s32[6,2,512]{2,1,0:T(2,128)S(1)}, s32[6,2,512]{2,1,0:T(2,128)S(1)}, u32[]{:S(2)}, u32[]{:S(2)}) collective-permute-start(s32[6,2,512]{2,1,0:T(2,128)S(1)} %get-tuple-element.48), channel_id=1, source_target_pairs={{0,4},{1,6},{2,12},{3,14},{4,21},{5,23},{6,29},{7,31},{8,36},{9,38... | collective-permute-start | bytes 73736 | tf_op jit(solution)/shard_map/ppermute | solution.py:250
  27.5 15.8 %copy-start.6 = (f32[1,768]{1,0:T(1,128)}, f32[1,768]{1,0:T(1,128)S(1)}, u32[]{:S(2)}) copy-start(f32[1,768]{1,0:T(1,128)S(1)} %collective-permute-done.1.far_gate_ref) | copy-start | bytes 9220
  27.5 15.8 %collective-permute-start.5 = (s32[6,2,512]{2,1,0:T(2,128)S(1)}, s32[6,2,512]{2,1,0:T(2,128)S(1)}, u32[]{:S(2)}, u32[]{:S(2)}) collective-permute-start(s32[6,2,512]{2,1,0:T(2,128)S(1)} %get-tuple-element.45), channel_id=1, source_target_pairs={{0,6},{1,4},{2,14},{3,12},{4,23},{5,21},{6,31},{7,29},{8,38},{9,36... | collective-permute-start | bytes 73736 | tf_op jit(solution)/shard_map/ppermute | solution.py:250
  43.3 0.7 copy-start.4
  44.0 91.3 %all-to-all-start = ((bf16[128,2,16,768]{3,2,1,0:T(8,128)(2,1)}), bf16[128,2,16,768]{3,2,1,0:T(8,128)(2,1)}, u32[]{:S(2)}, u32[]{:S(2)}) async-start(bf16[128,2,16,768]{3,2,1,0:T(8,128)(2,1)} %bitcast.38), calls=%async_computation | async-start | bytes 12582912 | tf_op jit(solution)/shard_map/all_to_all | solution.py:310
  55.1 99.9 %all-gather.2.cloned.1.call-start = ((), (), s32[]{:S(2)}) async-start(), calls=%async_computation.3 | async-start | bytes 2506752 | tf_op jit(solution)/shard_map/all_gather | solution.py:309
  143.9 52.6 %all-to-all-start.2 = ((bf16[64,16,1536]{2,1,0:T(8,128)(2,1)}), bf16[64,16,1536]{2,1,0:T(8,128)(2,1)}, u32[]{:S(2)}, u32[]{:S(2)}) async-start(bf16[64,16,1536]{2,1,0:T(8,128)(2,1)} %second_mix.3), calls=%async_computation.2 | async-start | bytes 6291456 | tf_op jit(solution)/shard_map/all_to_all | solution.py:330
  155.1 61.9 %collective-permute-start.7 = (bf16[768,1536]{1,0:T(8,128)(2,1)}, bf16[768,1536]{1,0:T(8,128)(2,1)}, u32[]{:S(2)}, u32[]{:S(2)}) collective-permute-start(bf16[768,1536]{1,0:T(8,128)(2,1)} %all-gather.2.cloned.1.call-done), channel_id=1, source_target_pairs={{0,2},{2,0},{4,6},{6,4},{8,10},{10,8},{12,14},{14,12},{16,18},{18,... | collective-permute-start | bytes 7077896 | tf_op jit(solution)/shard_map/ppermute | solution.py:231
  196.5 81.0 %all-to-all-start.1 = ((bf16[64,16,1536]{2,1,0:T(8,128)(2,1)}), bf16[64,16,1536]{2,1,0:T(8,128)(2,1)}, u32[]{:S(2)}, u32[]{:S(2)}) async-start(bf16[64,16,1536]{2,1,0:T(8,128)(2,1)} %second_mix.2), calls=%async_computation.1 | async-start | bytes 6291456 | tf_op jit(solution)/shard_map/all_to_all | solution.py:330
  202.8 5.5 %copy-start.3 = (bf16[2,384,4,384]{3,2,1,0:T(4,128)(2,1)S(1)}, bf16[2,384,4,384]{3,2,1,0:T(4,128)(2,1)}, u32[]{:S(2)}) copy-start(bf16[2,384,4,384]{3,2,1,0:T(4,128)(2,1)} %param.16) | copy-start | bytes 7077892
  208.2 35.8 %collective-permute-start.8 = (bf16[8,128,768]{2,1,0:T(8,128)(2,1)}, bf16[8,128,768]{2,1,0:T(8,128)(2,1)}, u32[]{:S(2)}, u32[]{:S(2)}) collective-permute-start(bf16[8,128,768]{2,1,0:T(8,128)(2,1)} %get-tuple-element.30), channel_id=1, source_target_pairs={{0,1},{1,0},{2,3},{3,2},{4,5},{5,4},{6,7},{7,6},{8,9},{9,8},{10,11... | collective-permute-start | bytes 4718600 | tf_op jit(solution)/shard_map/ppermute | solution.py:227
  215.7 61.8 %collective-permute-start.6 = (bf16[8,128,768]{2,1,0:T(8,128)(2,1)}, bf16[8,128,768]{2,1,0:T(8,128)(2,1)S(1)}, u32[]{:S(2)}, u32[]{:S(2)}) collective-permute-start(bf16[8,128,768]{2,1,0:T(8,128)(2,1)} %get-tuple-element.27), channel_id=1, source_target_pairs={{0,1},{1,0},{2,3},{3,2},{4,5},{5,4},{6,7},{7,6},{8,9},{9,8},{10,11... | collective-permute-start | bytes 4718600 | tf_op jit(solution)/shard_map/ppermute | solution.py:227
  258.4 50.7 %collective-permute-start.9 = (bf16[8,64,768]{2,1,0:T(8,128)(2,1)}, bf16[8,64,768]{2,1,0:T(8,128)(2,1)S(1)}, u32[]{:S(2)}, u32[]{:S(2)}) collective-permute-start(bf16[8,64,768]{2,1,0:T(8,128)(2,1)} %get-tuple-element.35), channel_id=1, source_target_pairs={{0,1},{1,0},{2,3},{3,2},{4,5},{5,4},{6,7},{7,6},{8,9},{9,8},{10,11... | collective-permute-start | bytes 2359304 | tf_op jit(solution)/shard_map/ppermute | solution.py:227
  273.0 38.3 %collective-permute-start.10 = (bf16[8,64,768]{2,1,0:T(8,128)(2,1)}, bf16[8,64,768]{2,1,0:T(8,128)(2,1)}, u32[]{:S(2)}, u32[]{:S(2)}) collective-permute-start(bf16[8,64,768]{2,1,0:T(8,128)(2,1)} %get-tuple-element.36), channel_id=1, source_target_pairs={{0,1},{1,0},{2,3},{3,2},{4,5},{5,4},{6,7},{7,6},{8,9},{9,8},{10,11... | collective-permute-start | bytes 2359304 | tf_op jit(solution)/shard_map/ppermute | solution.py:227
  277.5 1.2 copy-start.2
  293.2 34.9 %collective-permute-start.11 = (bf16[8,64,768]{2,1,0:T(8,128)(2,1)}, bf16[8,64,768]{2,1,0:T(8,128)(2,1)S(1)}, u32[]{:S(2)}, u32[]{:S(2)}) collective-permute-start(bf16[8,64,768]{2,1,0:T(8,128)(2,1)} %get-tuple-element.37), channel_id=1, source_target_pairs={{0,1},{1,0},{2,3},{3,2},{4,5},{5,4},{6,7},{7,6},{8,9},{9,8},{10,11... | collective-permute-start | bytes 2359304 | tf_op jit(solution)/shard_map/ppermute | solution.py:227
  307.8 37.1 %collective-permute-start.12 = (bf16[8,64,768]{2,1,0:T(8,128)(2,1)}, bf16[8,64,768]{2,1,0:T(8,128)(2,1)S(1)}, u32[]{:S(2)}, u32[]{:S(2)}) collective-permute-start(bf16[8,64,768]{2,1,0:T(8,128)(2,1)} %get-tuple-element.38), channel_id=1, source_target_pairs={{0,1},{1,0},{2,3},{3,2},{4,5},{5,4},{6,7},{7,6},{8,9},{9,8},{10,11... | collective-permute-start | bytes 2359304 | tf_op jit(solution)/shard_map/ppermute | solution.py:227
  309.1 36.7 %copy-start.1 = (bf16[512,512]{1,0:T(8,128)(2,1)S(1)}, bf16[512,512]{1,0:T(8,128)(2,1)}, u32[]{:S(2)}) copy-start(bf16[512,512]{1,0:T(8,128)(2,1)} %param.13) | copy-start | bytes 1572868
Sparse Core Ops, SparseCore 0:
  58.2 84.5 all-gather.1

commit v3 on v2

v3 whole, which is shorter than its diff:
```python
import jax
import jax.numpy as jnp
import numpy as np
from jax import lax
from jax.experimental import pallas as pl
from jax.experimental.pallas import tpu as pltpu
from jax.sharding import PartitionSpec as P


BLK = 128
HALF = 768
BW = 384
WIDE = 1536
VMEM = 56 * 1024 * 1024
BOTH = ("ctx", "ch")
N_CTX = 64


def z_hi(i):
    return (i // 8) % 2


SIDES = [[2 * i + (s ^ z_hi(i)) for i in range(N_CTX)] for s in range(2)]
PLANES = [[i for i in range(N_CTX) if z_hi(i) == z and i % 2 == core] for z in range(2) for core in range(2)]


def limits(exponent):
    return lax.shift_left(jnp.ones_like(exponent), exponent + 9).astype(jnp.float32) * 0.875


def regroup_matrix():
    matrix = np.zeros((256, 256), np.float32)
    for i in range(16):
        for r in range(2):
            for a in range(8):
                matrix[i * 16 + r * 8 + a, a * 32 + i * 2 + r] = 1.0
    return matrix


def first_kernel(mix_ref, perm_ref, tok_ref, spec_ref, exp_ref, out_ref, enc_ref):
    columns = limits(exp_ref[0]).T
    mix = mix_ref[...]
    for pair in range(4):
        rhs = jnp.concatenate([tok_ref[2 * pair], tok_ref[2 * pair + 1]], axis=1)
        acc = jnp.dot(mix, rhs, preferred_element_type=jnp.float32)
        for side in range(2):
            a = 2 * pair + side
            value = acc[:, side * BLK:(side + 1) * BLK] * spec_ref[a].astype(jnp.float32)
            top = columns[:, a:a + 1]
            enc_ref[a] = jnp.clip(value, -top, top).astype(jnp.bfloat16)
    for g in range(4):
        for h in range(2):
            both = jnp.concatenate(
                [
                    enc_ref[:, s * 256 + h * 128 + g * 32:s * 256 + h * 128 + (g + 1) * 32, :].reshape(256, BLK)
                    for s in range(2)
                ],
                axis=1,
            )
            moved = jnp.dot(perm_ref[...], both, preferred_element_type=jnp.float32).astype(jnp.bfloat16)
            for s in range(2):
                cols = slice(s * BLK, (s + 1) * BLK)
                out_ref[g * 16:g * 16 + 8, s, h] = moved[:128, cols].reshape(8, 16, BLK)
                out_ref[g * 16 + 8:g * 16 + 16, 1 - s, h] = moved[128:, cols].reshape(8, 16, BLK)


def first_stage(mix_first, perm, tokens, spectral, exponents):
    wide = pl.BlockSpec((8, 512, BLK), lambda d: (0, 0, d))
    return pl.pallas_call(
        first_kernel,
        grid=(HALF // BLK,),
        in_specs=[
            pl.BlockSpec((512, 512), lambda d: (0, 0)),
            pl.BlockSpec((256, 256), lambda d: (0, 0)),
            wide,
            wide,
            pl.BlockSpec((1, 8, 512), lambda d: (d, 0, 0)),
        ],
        out_specs=pl.BlockSpec((N_CTX, 2, 2, 16, BLK), lambda d: (0, 0, 0, 0, d)),
        out_shape=jax.ShapeDtypeStruct((N_CTX, 2, 2, 16, HALF), jnp.bfloat16),
        scratch_shapes=[pltpu.VMEM((8, 512, BLK), jnp.bfloat16)],
        compiler_params=pltpu.CompilerParams(vmem_limit_bytes=VMEM),
        cost_estimate=pl.CostEstimate(flops=4_800_000_000, bytes_accessed=18_900_000, transcendentals=0),
        name="first_mix",
    )(mix_first, perm, tokens, spectral, exponents)


def second_kernel(mix_ref, recv_ref, exp_ref, out_ref):
    columns = limits(exp_ref[0, 0]).T
    mix = mix_ref[...]
    both = recv_ref[:, 0, 0].astype(jnp.float32)
    parts = []
    for r in range(2):
        right = both[:, r * 8:(r + 1) * 8, :].reshape(512, HALF).astype(jnp.bfloat16)
        parts.append(jnp.dot(mix, right, preferred_element_type=jnp.float32))
    for n in range(6):
        cols = slice(n * BLK, (n + 1) * BLK)
        held = []
        for r in range(2):
            top = columns[:, 2 * n + r:2 * n + r + 1]
            held.append(jnp.clip(parts[r][:, cols], -top, top).reshape(N_CTX, 8, BLK))
        out_ref[:, :, cols] = jnp.concatenate(held, axis=1).astype(jnp.bfloat16)


def second_stage(mix, received, exponents, h):
    return pl.pallas_call(
        second_kernel,
        grid=(2,),
        in_specs=[
            pl.BlockSpec((512, 512), lambda c: (0, 0)),
            pl.BlockSpec((N_CTX, 1, 1, 16, HALF), lambda c: (0, c, h, 0, 0)),
            pl.BlockSpec((1, 1, 12, 512), lambda c: (h, c, 0, 0)),
        ],
        out_specs=pl.BlockSpec((N_CTX, 16, HALF), lambda c: (0, 0, c)),
        out_shape=jax.ShapeDtypeStruct((N_CTX, 16, WIDE), jnp.bfloat16),
        compiler_params=pltpu.CompilerParams(vmem_limit_bytes=VMEM),
        cost_estimate=pl.CostEstimate(flops=1_600_000_000, bytes_accessed=7_000_000, transcendentals=0),
        name="second_mix",
    )(mix, received, exponents)


def mixer_kernel(
    place_ref, perm_ref, recv_ref, own_tok_ref, far_tok_ref, gate_ref, up_ref, down_ref, *rest
):
    own_out_ref, far_out_ref, gated_ref, total_ref = rest[-4:]
    c = place_ref[1]
    p = pl.program_id(0)
    q = pl.program_id(1)

    def gate_half(half, tok_ref):
        start = pl.multiple_of((c if half == 0 else 1 - c) * HALF, BLK)
        for g in range(2):
            mixed = jnp.dot(
                perm_ref[...],
                recv_ref[g * 16:(g + 1) * 16, :, pl.ds(start, HALF)].reshape(256, HALF),
                preferred_element_type=jnp.float32,
            )
            tok = tok_ref[:, g * 32:(g + 1) * 32, :].reshape(256, HALF).astype(jnp.float32)
            slope = jax.nn.sigmoid(tok * gate_ref[half:half + 1, :])
            gated_ref[half, g * 256:(g + 1) * 256, :] = (tok + mixed * slope).astype(jnp.bfloat16)

    @pl.when((p == 0) & (q == 0))
    def _():
        gate_half(0, own_tok_ref)

    @pl.when((p == 1) & (q == 0))
    def _():
        gate_half(1, far_tok_ref)

    hidden = []
    for i in range(2):
        pre = jnp.dot(
            gated_ref[p, :, i * BW:(i + 1) * BW], up_ref[0, i], preferred_element_type=jnp.float32
        )
        hidden.append(jax.nn.gelu(pre, approximate=True).astype(jnp.bfloat16))
    parts = []
    for k in range(2):
        cols = slice(k * BW, (k + 1) * BW)
        left = jnp.concatenate([part[:, cols] for part in hidden], axis=1)
        right = down_ref[0, :, :, cols].reshape(HALF, BW)
        parts.append(jnp.dot(left, right, preferred_element_type=jnp.float32))

    @pl.when(p == 0)
    def _():
        for k in range(2):
            total_ref[q, :, k * BW:(k + 1) * BW] = parts[k]

    def finish(half, out_ref):
        for k in range(2):
            cols = slice(k * BW, (k + 1) * BW)
            result = gated_ref[half, :, cols].astype(jnp.float32) + total_ref[half, :, cols] + parts[k]
            result = result.astype(jnp.bfloat16)
            for g in range(2):
                out_ref[:, g * 32:(g + 1) * 32, cols] = result[g * 256:(g + 1) * 256].reshape(8, 32, BW)

    @pl.when((p == 1) & (q == 0))
    def _():
        finish(0, own_out_ref)

    @pl.when((p == 1) & (q == 1))
    def _():
        finish(1, far_out_ref)


def mixer_stage(place, perm, received, tokens, far_tokens, gates, ups, downs, whole, n):
    weight = pl.BlockSpec((1, 2, BW, HALF), lambda p, q, place: (p, 0, 0, (place[1] + q) % 2))
    own = pl.BlockSpec((8, 64, HALF), lambda p, q, place: (0, 4 * place[0] + n, 0))
    far = pl.BlockSpec((8, 64, HALF), lambda p, q, place: (0, 0, 0))
    far_in = pl.BlockSpec((8, 64, HALF), lambda p, q, place: (0, 0, 0))
    in_specs = [
        pl.BlockSpec((256, 256), lambda p, q, place: (0, 0)),
        pl.BlockSpec((32, 16, WIDE), lambda p, q, place: (n % 2, 0, 0)),
        own,
        far_in,
        pl.BlockSpec((2, HALF), lambda p, q, place: (0, 0)),
        weight,
        weight,
    ]
    operands = [perm, received, tokens, far_tokens, gates, ups, downs]
    aliases = {}
    if whole is not None:
        aliases = {len(operands) + 1: 0}
        in_specs.append(pl.BlockSpec(memory_space=pl.ANY))
        operands.append(whole)
    return pl.pallas_call(
        mixer_kernel,
        grid_spec=pltpu.PrefetchScalarGridSpec(
            num_scalar_prefetch=1,
            grid=(2, 2),
            in_specs=in_specs,
            out_specs=[own, far],
            scratch_shapes=[
                pltpu.VMEM((2, 512, HALF), jnp.bfloat16),
                pltpu.VMEM((2, 512, HALF), jnp.float32),
            ],
        ),
        out_shape=[
            jax.ShapeDtypeStruct((8, 512, HALF), jnp.bfloat16),
            jax.ShapeDtypeStruct((8, 64, HALF), jnp.bfloat16),
        ],
        input_output_aliases=aliases,
        compiler_params=pltpu.CompilerParams(vmem_limit_bytes=VMEM),
        cost_estimate=pl.CostEstimate(
            flops=5_200_000_000, bytes_accessed=16_000_000, transcendentals=4_000_000
        ),
        name="channel_mix",
    )(place, *operands)


def swap(value):
    return lax.ppermute(value, "ch", [(0, 1), (1, 0)])


def swap_cores(value):
    return lax.ppermute(value, "ctx", [(i, i ^ 1) for i in range(N_CTX)])


def exponent_route(step):
    pairs = []
    for i0 in range(N_CTX):
        for c0 in range(2):
            s, h = i0 // 32, (i0 // 16) % 2
            i = 4 * (i0 % 16) + ((2 * h + c0) ^ step)
            pairs.append((2 * i0 + c0, 2 * i + (s ^ z_hi(i))))
    return pairs


def routed_exponents(second_exponents, ctx, ch):
    columns = second_exponents.transpose(2, 1, 0)
    source = 2 * ((ctx // 16) % 2) + ch
    got = []
    for step in range(4):
        rows = lax.dynamic_slice_in_dim(columns, 2 * (source ^ step), 2, 1)
        got.append(lax.ppermute(rows, BOTH, exponent_route(step)))

    def finish():
        stacked = jnp.stack(got)
        ordered = jnp.stack(
            [lax.dynamic_index_in_dim(stacked, v ^ (ctx % 4), 0, keepdims=False) for v in range(4)]
        )
        return ordered.reshape(2, 2, 12, 512)

    return got, finish


def body(
    tokens,
    mix_first,
    mix_second,
    spectral_kernel,
    gate_scale,
    up_weight,
    down_weight,
    first_exponents,
    second_exponents,
):
    ctx = lax.axis_index("ctx")
    ch = lax.axis_index("ch")
    core = ctx % 2
    side = ch ^ ((ctx // 8) % 2)
    place = jnp.stack([side, ch]).astype(jnp.int32)
    perm = regroup_matrix()

    rows = 2 * BW
    piece = rows // 16
    start = ((ctx // 16) * 4 + (ctx % 8) // 2) * piece
    cut = lambda w: lax.dynamic_slice_in_dim(w.reshape(rows, 4, BW), start, piece, 0).reshape(piece, WIDE)
    slice_far = swap(jnp.where(core == 0, cut(up_weight), cut(down_weight)))
    own_gate = gate_scale.reshape(1, HALF)
    far_gate = swap(own_gate)
    exps, finish_exps = routed_exponents(second_exponents, ctx, ch)

    send = first_stage(
        mix_first,
        jnp.asarray(perm, jnp.bfloat16),
        tokens,
        spectral_kernel,
        first_exponents.transpose(2, 0, 1),
    )
    send, slice_far, far_gate = lax.optimization_barrier((send, slice_far, far_gate))
    gathered = lax.all_gather(slice_far, "ctx", axis=0, tiled=True, axis_index_groups=PLANES)
    received = lax.all_to_all(
        send.reshape(128, 2, 16, HALF), BOTH, split_axis=0, concat_axis=0, tiled=True
    ).reshape(N_CTX, 2, 2, 16, HALF)

    whole_shape = (2, BW, WIDE)
    gates = jnp.concatenate([own_gate, far_gate], axis=0)
    tops = finish_exps()
    own_up = up_weight.reshape(whole_shape)
    own_down = down_weight.reshape(whole_shape)

    peel = lambda n: lax.dynamic_slice_in_dim(tokens, (1 - side) * 256 + 64 * n, 64, 1)
    far_tokens = [swap(peel(0))]
    peeled = [peel(n) for n in range(1, 4)]
    received, far_tokens[0], peeled, own_up, own_down, tops, gates = lax.optimization_barrier(
        (received, far_tokens[0], peeled, own_up, own_down, tops, gates)
    )
    far_tokens += [swap(part) for part in peeled]

    second = [second_stage(mix_second, received, tops, h) for h in range(2)]
    mixed0 = lax.all_to_all(
        second[0], BOTH, split_axis=0, concat_axis=0, tiled=True, axis_index_groups=SIDES
    )
    gathered, _ = lax.optimization_barrier((gathered, second[0]))
    crossed = swap_cores(gathered)
    far_up = jnp.where(core == 0, gathered, crossed).reshape(whole_shape)
    far_down = jnp.where(core == 0, crossed, gathered).reshape(whole_shape)
    ups = jnp.stack([own_up, far_up])
    downs = jnp.stack([own_down, far_down])
    mixed0, ups, downs, second[1], far_tokens[1], far_tokens[2] = lax.optimization_barrier(
        (mixed0, ups, downs, second[1], far_tokens[1], far_tokens[2])
    )
    mixed1 = lax.all_to_all(
        second[1], BOTH, split_axis=0, concat_axis=0, tiled=True, axis_index_groups=SIDES
    )
    whole = None
    back = []
    perm_back = jnp.asarray(perm.T, jnp.bfloat16)

    def place_part(whole, n):
        return lax.dynamic_update_slice_in_dim(whole, back[n], (1 - side) * 256 + 64 * n, 1)

    for n in range(4):
        if n == 3:
            whole = place_part(whole, 0)
        whole, far = mixer_stage(
            place, perm_back, (mixed0, mixed1)[n // 2], tokens, far_tokens[n], gates, ups, downs, whole, n
        )
        back.append(swap(far))
    for n in range(1, 4):
        whole = place_part(whole, n)
    return whole


def solution(mesh):
    placed = (
        P("ctx", None, "ch"),
        P(),
        P(),
        P("ctx", None, "ch"),
        P("ch"),
        P("ch", None, None, None),
        P("ch", None, None, None),
        P("ctx", None, "ch"),
        P(None, "ctx", "ch"),
    )
    return jax.shard_map(
        body, mesh=mesh, in_specs=placed, out_specs=P("ctx", None, "ch"), check_vma=False
    )
```

time: 354 us -> 290 us (0.82)
  waiting for transfers between devices: 156 us -> 114 us
  Pallas kernels: 92.9 us -> 77.6 us
  matrix products: 5.17 us -> 0 us
  local copies, waits for them, and re-layouts: 23.7 us -> 18.9 us
    all_to_all x1, waiting for transfers between devices: 66.4 us -> 0.01 us  [body(): lax.all_to_all(send.reshape(128, 2, 16, HALF), BOTH, split_axis=0, concat...]
    ppermute x4, waiting for transfers between devices: 0.01 us -> 56.5 us  [routed_exponents(): got.append(lax.ppermute(rows, BOTH, exponent_route(step)))]
    ppermute x8 -> x10, waiting for transfers between devices: 57.1 us -> 39 us  [swap(): return lax.ppermute(value, 'ch', [(0, 1), (1, 0)])]
    all_to_all x2, waiting for transfers between devices: 32.2 us -> 17.4 us  [the longest x1 11.8 us: body(): lax.all_to_all(second[1], BOTH, split_axis=0, concat_axis=0, tiled=True,...]
    pallas_call x3 -> x2, Pallas kernels: 22.6 us -> 10 us  [second_stage(): pl.pallas_call(second_kernel, grid=(2,), in_specs=[pl.BlockSpec((512, 512...]
    reshape x4 -> x3, local copies, waits for them, and re-layouts: 12.7 us -> 7.47 us  [the longest x1 5.04 us: body(): own_down = down_weight.reshape(whole_shape)]
    dot_general x2 -> x0, matrix products: 5.17 us -> none  [the longest x1 3.17 us: doubled_mix(): lax.dot_general(tall, pick, (((1,), (1,)), ((), ())), preferred_element_t...]
    another operation x0 -> x1, other arithmetic: none -> 3.91 us  [body(): ups = jnp.stack([own_up, far_up])]
  transfers between devices with their start and end apart: 17 -> 19, of which waited for: 7 -> 7; matrix products, arithmetic and copies ran while one was open for 9% -> 8% of each run, Pallas kernels for 26% -> 27%
where the time goes in v3:
time: 290 us; the launch traced here: 289 us
  waiting for transfers between devices  114 us (39%)
  Pallas kernels  77.6 us (27%)
  starting transfers between devices  56.8 us (20%)
  local copies, waits for them, and re-layouts  18.9 us (7%)
  between operations  13.7 us (5%)
  other arithmetic  8.28 us (3%)
    ppermute x4, waiting for transfers between devices, routed_exponents(): got.append(lax.ppermute(rows, BOTH, exponent_route(step)))  56.5 us
    pallas_call x4, Pallas kernels, mixer_stage(): pl.pallas_call(mixer_kernel, grid_spec=pltpu.PrefetchScalarGridSpec(num_s...  55.3 us
    ppermute x10, waiting for transfers between devices, swap(): return lax.ppermute(value, 'ch', [(0, 1), (1, 0)])  39 us
    ppermute x4, starting transfers between devices, routed_exponents(): got.append(lax.ppermute(rows, BOTH, exponent_route(step)))  18.9 us
    pallas_call x1, Pallas kernels, first_stage(): pl.pallas_call(first_kernel, grid=(HALF // BLK,), in_specs=[pl.BlockSpec(...  12.4 us
    all_to_all x1, waiting for transfers between devices, body(): lax.all_to_all(second[1], BOTH, split_axis=0, concat_axis=0, tiled=True,...  11.8 us
    all_to_all x1, starting transfers between devices, body(): lax.all_to_all(second[0], BOTH, split_axis=0, concat_axis=0, tiled=True,...  11.6 us
    all_to_all x1, starting transfers between devices, body(): lax.all_to_all(send.reshape(128, 2, 16, HALF), BOTH, split_axis=0, concat...  11.4 us
  transfers between devices with their start and end apart: 19, of which 7 were waited for; matrix products, arithmetic and copies ran while one was open for 8% of the time, Pallas kernels for 27%

profile of v3, /device:TPU:1, one launch (start us, length us, event | category | flops | bytes accessed | tf_op | source)
XLA Modules:
  0.0 288.8 jit_solution(18405976342460630990)
XLA Ops:
  6.5 0.7 reshape.30
  7.2 2.5 collective-permute-start.1
  9.7 1.1 dynamic-slice_select_fusion
  10.8 0.1 collective-permute-start
  10.9 12.4 %first_mix.1 = bf16[64,2,2,16,768]{4,3,2,1,0:T(8,128)(2,1)} custom-call(bf16[512,512]{1,0:T(8,128)(2,1)} %mix_ref.3, bf16[256,256]{1,0:T(8,128)(2,1)} %constant.123.clone.perm_ref, bf16[8,512,768]{2,1,0:T(8,128)(2,1)} %own_tok_ref.7, bf16[8,512,768]{2,1,0:T(8,128)(2,1)} %spec_ref.1, s32[6,8,512]{2,1,0:T(8,128)} %bitcast.36), custom_call_target="tpu_custom_call" | custom-call | flops 4800000000 | bytes 18900000 | tf_op jit(solution)/shard_map/first_mix/pallas_call | solution.py:69
  23.2 0.0 collective-permute-done.1
  23.2 0.0 collective-permute-done
  23.3 0.7 copy-done.7
  23.9 11.4 %all-to-all-start = ((bf16[128,2,16,768]{3,2,1,0:T(8,128)(2,1)}), bf16[128,2,16,768]{3,2,1,0:T(8,128)(2,1)}, u32[]{:S(2)}, u32[]{:S(2)}) async-start(bf16[128,2,16,768]{3,2,1,0:T(8,128)(2,1)} %bitcast.27), calls=%async_computation | async-start | bytes 12582912 | tf_op jit(solution)/shard_map/all_to_all | solution.py:302
  35.3 0.0 copy-start.8
  35.4 0.0 copy-start.3
  35.4 0.0 all-gather.2.cloned.1.call-start
  35.4 0.7 all-gather.2.cloned.1.call-update
  36.2 3.6 %constant_dynamic-slice_fusion.4 = (bf16[8,64,768]{2,1,0:T(8,128)(2,1)}, bf16[8,64,768]{2,1,0:T(8,128)(2,1)}, bf16[8,64,768]{2,1,0:T(8,128)(2,1)}, bf16[8,64,768]{2,1,0:T(8,128)(2,1)}) fusion(bf16[8,512,768]{2,1,0:T(8,128)(2,1)} %own_tok_ref.7, s32[]{:T(128)S(6)} %select_n.121, s32[]{:T(128)S(6)} %select_n.120, s32[]{:T(128)S(6)} %select_n.119, s32[]{:T(128)S(6)} %select_n.118), kind=kLoop, calls=%fused_computation.20 | loop fusion | bytes 6291472 | tf_op jit(solution)/shard_map/dynamic_slice | solution.py:312
  39.7 1.5 collective-permute-start.2
  41.3 5.3 %collective-permute-start.3 = (s32[6,2,512]{2,1,0:T(2,128)S(1)}, s32[6,2,512]{2,1,0:T(2,128)S(1)}, u32[]{:S(2)}, u32[]{:S(2)}) collective-permute-start(s32[6,2,512]{2,1,0:T(2,128)S(1)} %get-tuple-element.69), channel_id=1, source_target_pairs={{0,0},{1,2},{2,8},{3,10},{4,17},{5,19},{6,25},{7,27},{8,32},{9,34}... | collective-permute-start | bytes 73736 | tf_op jit(solution)/shard_map/ppermute | solution.py:254
  46.6 3.1 %collective-permute-start.4 = (s32[6,2,512]{2,1,0:T(2,128)S(1)}, s32[6,2,512]{2,1,0:T(2,128)S(1)}, u32[]{:S(2)}, u32[]{:S(2)}) collective-permute-start(s32[6,2,512]{2,1,0:T(2,128)S(1)} %get-tuple-element.70), channel_id=1, source_target_pairs={{0,2},{1,0},{2,10},{3,8},{4,19},{5,17},{6,27},{7,25},{8,34},{9,32}... | collective-permute-start | bytes 73736 | tf_op jit(solution)/shard_map/ppermute | solution.py:254
  49.7 6.0 %collective-permute-start.6 = (s32[6,2,512]{2,1,0:T(2,128)S(1)}, s32[6,2,512]{2,1,0:T(2,128)S(1)}, u32[]{:S(2)}, u32[]{:S(2)}) collective-permute-start(s32[6,2,512]{2,1,0:T(2,128)S(1)} %get-tuple-element.71), channel_id=1, source_target_pairs={{0,6},{1,4},{2,14},{3,12},{4,23},{5,21},{6,31},{7,29},{8,38},{9,36... | collective-permute-start | bytes 73736 | tf_op jit(solution)/shard_map/ppermute | solution.py:254
  55.7 4.6 %collective-permute-start.5 = (s32[6,2,512]{2,1,0:T(2,128)S(1)}, s32[6,2,512]{2,1,0:T(2,128)S(1)}, u32[]{:S(2)}, u32[]{:S(2)}) collective-permute-start(s32[6,2,512]{2,1,0:T(2,128)S(1)} %get-tuple-element.72), channel_id=1, source_target_pairs={{0,4},{1,6},{2,12},{3,14},{4,21},{5,23},{6,29},{7,31},{8,36},{9,38... | collective-permute-start | bytes 73736 | tf_op jit(solution)/shard_map/ppermute | solution.py:254
  60.3 2.4 reshape.33
  62.7 5.0 %reshape.34 = bf16[2,384,1536]{2,1,0:T(8,128)(2,1)} reshape(bf16[2,384,4,384]{3,2,1,0:T(4,128)(2,1)} %param.17) | data formatting | bytes 4718592 | tf_op jit(solution)/shard_map/reshape | solution.py:310
  67.7 56.5 %collective-permute-done.3 = s32[6,2,512]{2,1,0:T(2,128)S(1)} collective-permute-done((s32[6,2,512]{2,1,0:T(2,128)S(1)}, s32[6,2,512]{2,1,0:T(2,128)S(1)}, u32[]{:S(2)}, u32[]{:S(2)}) %collective-permute-start.3) | collective-permute-done | bytes 24608 | tf_op jit(solution)/shard_map/ppermute | solution.py:254
  124.1 0.0 collective-permute-done.4
  124.2 0.0 collective-permute-done.6
  124.2 0.0 collective-permute-done.5
  124.3 0.1 reshape.35
  124.4 0.6 pad_maximum_fusion.2.gate_ref
  125.0 0.0 collective-permute-done.2.far_tok_ref
  125.0 0.8 copy.16.exp_ref
  125.7 5.0 %second_mix.2 = bf16[64,16,1536]{2,1,0:T(8,128)(2,1)} custom-call(bf16[512,512]{1,0:T(8,128)(2,1)} %mix_ref.5, bf16[64,2,2,16,768]{4,3,2,1,0:T(8,128)(2,1)} %bitcast.6.recv_ref, s32[2,2,12,512]{3,2,1,0:T(8,128)} %copy.16.exp_ref), custom_call_target="tpu_custom_call" | custom-call | flops 1600000000 | bytes 7000000 | tf_op jit(solution)/shard_map/second_mix/pallas_call | solution.py:106
  130.7 0.6 collective-permute-start.7
  131.3 11.6 %all-to-all-start.1 = ((bf16[64,16,1536]{2,1,0:T(8,128)(2,1)}), bf16[64,16,1536]{2,1,0:T(8,128)(2,1)S(1)}, u32[]{:S(2)}, u32[]{:S(2)}) async-start(bf16[64,16,1536]{2,1,0:T(8,128)(2,1)} %second_mix.2), calls=%async_computation.1 | async-start | bytes 6291456 | tf_op jit(solution)/shard_map/all_to_all | solution.py:321
  142.9 0.5 collective-permute-start.8
  143.5 1.0 collective-permute-start.9
  144.5 5.0 %second_mix.3 = bf16[64,16,1536]{2,1,0:T(8,128)(2,1)} custom-call(bf16[512,512]{1,0:T(8,128)(2,1)} %mix_ref.5, bf16[64,2,2,16,768]{4,3,2,1,0:T(8,128)(2,1)} %bitcast.6.recv_ref, s32[2,2,12,512]{3,2,1,0:T(8,128)} %copy.16.exp_ref), custom_call_target="tpu_custom_call" | custom-call | flops 1600000000 | bytes 7000000 | tf_op jit(solution)/shard_map/second_mix/pallas_call | solution.py:106
  149.5 0.0 collective-permute-done.7
  149.5 2.1 broadcast_select_fusion
  151.6 0.2 copy-done.1
  151.9 0.7 copy-done.2
  152.6 3.9 %pad_maximum_fusion = (bf16[2,2,384,1536]{3,2,1,0:T(8,128)(2,1)}, bf16[2,2,384,1536]{3,2,1,0:T(8,128)(2,1)}) fusion(bf16[1,2,384,1536]{3,2,1,0:T(8,128)(2,1)S(1)} %bitcast.31, bf16[1,2,384,1536]{3,2,1,0:T(8,128)(2,1)S(1)} %bitcast.28, bf16[1,2,384,1536]{3,2,1,0:T(8,128)(2,1)S(1)} %bitcast.30, bf16[1,2,384,1536]{3,2,1,0:T(8,128)(2,1)S(1)} %bitcast.29), kind=kLoop, calls=%fused_computation | loop fusion | flops 4718592 | bytes 18874368 | tf_op jit(solution)/shard_map/stack | solution.py:328
  156.5 5.4 %collective-permute-done.8.far_tok_ref = bf16[8,64,768]{2,1,0:T(8,128)(2,1)S(1)} collective-permute-done((bf16[8,64,768]{2,1,0:T(8,128)(2,1)}, bf16[8,64,768]{2,1,0:T(8,128)(2,1)S(1)}, u32[]{:S(2)}, u32[]{:S(2)}) %collective-permute-start.8) | collective-permute-done | bytes 786464 | tf_op jit(solution)/shard_map/ppermute | solution.py:231
  161.9 0.9 copy-done.6
  162.8 16.1 %collective-permute-done.9.far_tok_ref = bf16[8,64,768]{2,1,0:T(8,128)(2,1)} collective-permute-done((bf16[8,64,768]{2,1,0:T(8,128)(2,1)}, bf16[8,64,768]{2,1,0:T(8,128)(2,1)}, u32[]{:S(2)}, u32[]{:S(2)}) %collective-permute-start.9) | collective-permute-done | bytes 786464 | tf_op jit(solution)/shard_map/ppermute | solution.py:231
  178.8 5.6 %all-to-all-done.1.recv_ref = bf16[64,16,1536]{2,1,0:T(8,128)(2,1)S(1)} async-done(((bf16[64,16,1536]{2,1,0:T(8,128)(2,1)}), bf16[64,16,1536]{2,1,0:T(8,128)(2,1)S(1)}, u32[]{:S(2)}, u32[]{:S(2)}) %all-to-all-start.1) | async-done | bytes 3145760 | tf_op jit(solution)/shard_map/all_to_all | solution.py:321
  184.4 5.7 %all-to-all-start.2 = ((bf16[64,16,1536]{2,1,0:T(8,128)(2,1)}), bf16[64,16,1536]{2,1,0:T(8,128)(2,1)}, u32[]{:S(2)}, u32[]{:S(2)}) async-start(bf16[64,16,1536]{2,1,0:T(8,128)(2,1)} %second_mix.3), calls=%async_computation.2 | async-start | bytes 6291456 | tf_op jit(solution)/shard_map/all_to_all | solution.py:333
  190.1 0.6 pad_add_fusion.2.place_ref
  190.7 0.0 collective-permute-start.10
  190.7 13.8 %channel_mix.4 = (bf16[8,512,768]{2,1,0:T(8,128)(2,1)}, bf16[8,64,768]{2,1,0:T(8,128)(2,1)}) custom-call(s32[2]{0:T(128)} %pad_add_fusion.2.place_ref, bf16[256,256]{1,0:T(8,128)(2,1)} %constant.124.clone.perm_ref, bf16[64,16,1536]{2,1,0:T(8,128)(2,1)} %copy-done, bf16[8,512,768]{2,1,0:T(8,128)(2,1)} %own_tok_ref.7, bf16[8,64,768]{2,1,0:T(8,128)(2,1)} %copy-done.5, ...), custom_call_target="tpu_custom_call" | custom-call | flops 5200000000 | bytes 16000000 | tf_op jit(solution)/shard_map/channel_mix/pallas_call | solution.py:205
  204.5 1.5 collective-permute-start.11
  206.0 13.8 %channel_mix.5 = (bf16[8,512,768]{2,1,0:T(8,128)(2,1)}, bf16[8,64,768]{2,1,0:T(8,128)(2,1)}) custom-call(s32[2]{0:T(128)} %pad_add_fusion.2.place_ref, bf16[256,256]{1,0:T(8,128)(2,1)} %constant.124.clone.perm_ref, bf16[64,16,1536]{2,1,0:T(8,128)(2,1)} %copy-done, bf16[8,512,768]{2,1,0:T(8,128)(2,1)} %own_tok_ref.7, ...), custom_call_target="tpu_custom_call", output_to_operand_aliasing={{0}: (8, {})} | custom-call | flops 5200000000 | bytes 16000000 | tf_op jit(solution)/shard_map/channel_mix/pallas_call | solution.py:205
  219.8 0.0 collective-permute-start.12
  219.8 11.8 %all-to-all-done.2.recv_ref = bf16[64,16,1536]{2,1,0:T(8,128)(2,1)} async-done(((bf16[64,16,1536]{2,1,0:T(8,128)(2,1)}), bf16[64,16,1536]{2,1,0:T(8,128)(2,1)}, u32[]{:S(2)}, u32[]{:S(2)}) %all-to-all-start.2) | async-done | bytes 3145760 | tf_op jit(solution)/shard_map/all_to_all | solution.py:333
  231.6 13.8 %channel_mix.6 = (bf16[8,512,768]{2,1,0:T(8,128)(2,1)}, bf16[8,64,768]{2,1,0:T(8,128)(2,1)}) custom-call(s32[2]{0:T(128)} %pad_add_fusion.2.place_ref, bf16[256,256]{1,0:T(8,128)(2,1)} %constant.124.clone.perm_ref, bf16[64,16,1536]{2,1,0:T(8,128)(2,1)} %all-to-all-done.2.recv_ref, bf16[8,512,768]{2,1,0:T(8,128)(2,1)} %own_tok_ref.7, ...), custom_call_target="tpu_custom_call", output_to_operand_aliasing={{0}: (8, {})} | custom-call | flops 5200000000 | bytes 16000000 | tf_op jit(solution)/shard_map/channel_mix/pallas_call | solution.py:205
  245.4 0.0 collective-permute-start.13
  245.4 0.0 collective-permute-done.11
  245.4 0.9 constant_dynamic-update-slice_fusion.3.rest_0_
  246.3 0.0 collective-permute-done.10.far_tok_ref
  246.4 13.8 %channel_mix.7 = (bf16[8,512,768]{2,1,0:T(8,128)(2,1)}, bf16[8,64,768]{2,1,0:T(8,128)(2,1)}) custom-call(s32[2]{0:T(128)} %pad_add_fusion.2.place_ref, bf16[256,256]{1,0:T(8,128)(2,1)} %constant.124.clone.perm_ref, bf16[64,16,1536]{2,1,0:T(8,128)(2,1)} %all-to-all-done.2.recv_ref, bf16[8,512,768]{2,1,0:T(8,128)(2,1)} %own_tok_ref.7, ...), custom_call_target="tpu_custom_call", output_to_operand_aliasing={{0}: (8, {})} | custom-call | flops 5200000000 | bytes 16000000 | tf_op jit(solution)/shard_map/channel_mix/pallas_call | solution.py:205
  260.2 1.5 collective-permute-start.14
  261.6 0.9 constant_dynamic-update-slice_fusion.2
  262.6 1.6 collective-permute-done.13
  264.2 0.9 constant_dynamic-update-slice_fusion.1
  265.1 15.9 %collective-permute-done.14 = bf16[8,64,768]{2,1,0:T(8,128)(2,1)S(1)} collective-permute-done((bf16[8,64,768]{2,1,0:T(8,128)(2,1)}, bf16[8,64,768]{2,1,0:T(8,128)(2,1)S(1)}, u32[]{:S(2)}, u32[]{:S(2)}) %collective-permute-start.14) | collective-permute-done | bytes 786464 | tf_op jit(solution)/shard_map/ppermute | solution.py:231
  281.1 0.9 constant_dynamic-update-slice_fusion
  (21 shorter events, 0.2 us)
Async XLA Ops:
  7.2 16.0 %collective-permute-start.1 = (f32[1,768]{1,0:T(1,128)S(1)}, f32[1,768]{1,0:T(1,128)S(1)}, u32[]{:S(2)}, u32[]{:S(2)}) collective-permute-start(f32[1,768]{1,0:T(1,128)S(1)} %reshape.30), channel_id=1, source_target_pairs={{0,1},{1,0},{2,3},{3,2},{4,5},{5,4},{6,7},{7,6},{8,9},{9,8},{10,11... | collective-permute-start | bytes 9224 | tf_op jit(solution)/shard_map/ppermute | solution.py:231
  10.8 12.5 %collective-permute-start = (bf16[48,1536]{1,0:T(8,128)(2,1)S(1)}, bf16[48,1536]{1,0:T(8,128)(2,1)S(1)}, u32[]{:S(2)}, u32[]{:S(2)}) collective-permute-start(bf16[48,1536]{1,0:T(8,128)(2,1)S(1)} %bitcast.35), channel_id=1, source_target_pairs={{0,1},{1,0},{2,3},{3,2},{4,5},{5,4},{6,7},{7,6},{8,9},{9,8},{10,11... | collective-permute-start | bytes 442376 | tf_op jit(solution)/shard_map/ppermute | solution.py:231
  23.3 0.7 copy-start.7
  23.9 101.1 %all-to-all-start = ((bf16[128,2,16,768]{3,2,1,0:T(8,128)(2,1)}), bf16[128,2,16,768]{3,2,1,0:T(8,128)(2,1)}, u32[]{:S(2)}, u32[]{:S(2)}) async-start(bf16[128,2,16,768]{3,2,1,0:T(8,128)(2,1)} %bitcast.27), calls=%async_computation | async-start | bytes 12582912 | tf_op jit(solution)/shard_map/all_to_all | solution.py:302
  35.3 5.9 %copy-start.8 = (s32[512,8,6]{0,1,2:T(8,128)S(1)}, s32[512,8,6]{0,1,2:T(8,128)}, u32[]{:S(2)}) copy-start(s32[512,8,6]{0,1,2:T(8,128)} %param.19) | copy-start | bytes 294916
  35.4 24.9 %copy-start.3 = (bf16[2,384,4,384]{3,2,1,0:T(4,128)(2,1)S(1)}, bf16[2,384,4,384]{3,2,1,0:T(4,128)(2,1)}, u32[]{:S(2)}) copy-start(bf16[2,384,4,384]{3,2,1,0:T(4,128)(2,1)} %param.16) | copy-start | bytes 7077892
  35.4 95.4 %all-gather.2.cloned.1.call-start = ((), (), s32[]{:S(2)}) async-start(), calls=%async_computation.3 | async-start | bytes 2506752 | tf_op jit(solution)/shard_map/all_gather | solution.py:301
  39.7 85.2 %collective-permute-start.2 = (bf16[8,64,768]{2,1,0:T(8,128)(2,1)}, bf16[8,64,768]{2,1,0:T(8,128)(2,1)S(1)}, u32[]{:S(2)}, u32[]{:S(2)}) collective-permute-start(bf16[8,64,768]{2,1,0:T(8,128)(2,1)} %get-tuple-element.62), channel_id=1, source_target_pairs={{0,1},{1,0},{2,3},{3,2},{4,5},{5,4},{6,7},{7,6},{8,9},{9,8},{10,11... | collective-permute-start | bytes 2359304 | tf_op jit(solution)/shard_map/ppermute | solution.py:231
  41.3 82.9 %collective-permute-start.3 = (s32[6,2,512]{2,1,0:T(2,128)S(1)}, s32[6,2,512]{2,1,0:T(2,128)S(1)}, u32[]{:S(2)}, u32[]{:S(2)}) collective-permute-start(s32[6,2,512]{2,1,0:T(2,128)S(1)} %get-tuple-element.69), channel_id=1, source_target_pairs={{0,0},{1,2},{2,8},{3,10},{4,17},{5,19},{6,25},{7,27},{8,32},{9,34}... | collective-permute-start | bytes 73736 | tf_op jit(solution)/shard_map/ppermute | solution.py:254
  46.6 77.6 %collective-permute-start.4 = (s32[6,2,512]{2,1,0:T(2,128)S(1)}, s32[6,2,512]{2,1,0:T(2,128)S(1)}, u32[]{:S(2)}, u32[]{:S(2)}) collective-permute-start(s32[6,2,512]{2,1,0:T(2,128)S(1)} %get-tuple-element.70), channel_id=1, source_target_pairs={{0,2},{1,0},{2,10},{3,8},{4,19},{5,17},{6,27},{7,25},{8,34},{9,32}... | collective-permute-start | bytes 73736 | tf_op jit(solution)/shard_map/ppermute | solution.py:254
  49.7 74.5 %collective-permute-start.6 = (s32[6,2,512]{2,1,0:T(2,128)S(1)}, s32[6,2,512]{2,1,0:T(2,128)S(1)}, u32[]{:S(2)}, u32[]{:S(2)}) collective-permute-start(s32[6,2,512]{2,1,0:T(2,128)S(1)} %get-tuple-element.71), channel_id=1, source_target_pairs={{0,6},{1,4},{2,14},{3,12},{4,23},{5,21},{6,31},{7,29},{8,38},{9,36... | collective-permute-start | bytes 73736 | tf_op jit(solution)/shard_map/ppermute | solution.py:254
  55.7 68.5 %collective-permute-start.5 = (s32[6,2,512]{2,1,0:T(2,128)S(1)}, s32[6,2,512]{2,1,0:T(2,128)S(1)}, u32[]{:S(2)}, u32[]{:S(2)}) collective-permute-start(s32[6,2,512]{2,1,0:T(2,128)S(1)} %get-tuple-element.72), channel_id=1, source_target_pairs={{0,4},{1,6},{2,12},{3,14},{4,21},{5,23},{6,29},{7,31},{8,36},{9,38... | collective-permute-start | bytes 73736 | tf_op jit(solution)/shard_map/ppermute | solution.py:254
  125.0 5.8 %copy-start.5 = (bf16[8,64,768]{2,1,0:T(8,128)(2,1)}, bf16[8,64,768]{2,1,0:T(8,128)(2,1)S(1)}, u32[]{:S(2)}) copy-start(bf16[8,64,768]{2,1,0:T(8,128)(2,1)S(1)} %collective-permute-done.2.far_tok_ref) | copy-start | bytes 2359300
  130.7 18.8 %collective-permute-start.7 = (bf16[768,1536]{1,0:T(8,128)(2,1)}, bf16[768,1536]{1,0:T(8,128)(2,1)}, u32[]{:S(2)}, u32[]{:S(2)}) collective-permute-start(bf16[768,1536]{1,0:T(8,128)(2,1)} %all-gather.2.cloned.1.call-done), channel_id=1, source_target_pairs={{0,2},{2,0},{4,6},{6,4},{8,10},{10,8},{12,14},{14,12},{16,18},{18,... | collective-permute-start | bytes 7077896 | tf_op jit(solution)/shard_map/ppermute | solution.py:235
  131.3 53.1 %all-to-all-start.1 = ((bf16[64,16,1536]{2,1,0:T(8,128)(2,1)}), bf16[64,16,1536]{2,1,0:T(8,128)(2,1)S(1)}, u32[]{:S(2)}, u32[]{:S(2)}) async-start(bf16[64,16,1536]{2,1,0:T(8,128)(2,1)} %second_mix.2), calls=%async_computation.1 | async-start | bytes 6291456 | tf_op jit(solution)/shard_map/all_to_all | solution.py:321
  142.9 6.6 %copy-start.4 = (bf16[768,1536]{1,0:T(8,128)(2,1)S(1)}, bf16[768,1536]{1,0:T(8,128)(2,1)}, u32[]{:S(2)}) copy-start(bf16[768,1536]{1,0:T(8,128)(2,1)} %all-gather.2.cloned.1.call-done) | copy-start | bytes 7077892
  142.9 19.0 %collective-permute-start.8 = (bf16[8,64,768]{2,1,0:T(8,128)(2,1)}, bf16[8,64,768]{2,1,0:T(8,128)(2,1)S(1)}, u32[]{:S(2)}, u32[]{:S(2)}) collective-permute-start(bf16[8,64,768]{2,1,0:T(8,128)(2,1)} %get-tuple-element.40), channel_id=1, source_target_pairs={{0,1},{1,0},{2,3},{3,2},{4,5},{5,4},{6,7},{7,6},{8,9},{9,8},{10,11... | collective-permute-start | bytes 2359304 | tf_op jit(solution)/shard_map/ppermute | solution.py:231
  143.5 35.4 %collective-permute-start.9 = (bf16[8,64,768]{2,1,0:T(8,128)(2,1)}, bf16[8,64,768]{2,1,0:T(8,128)(2,1)}, u32[]{:S(2)}, u32[]{:S(2)}) collective-permute-start(bf16[8,64,768]{2,1,0:T(8,128)(2,1)} %get-tuple-element.41), channel_id=1, source_target_pairs={{0,1},{1,0},{2,3},{3,2},{4,5},{5,4},{6,7},{7,6},{8,9},{9,8},{10,11... | collective-permute-start | bytes 2359304 | tf_op jit(solution)/shard_map/ppermute | solution.py:231
  149.5 2.4 copy-start.1
  149.5 3.1 %copy-start.2 = (bf16[2,384,1536]{2,1,0:T(8,128)(2,1)S(1)}, bf16[2,384,1536]{2,1,0:T(8,128)(2,1)}, u32[]{:S(2)}) copy-start(bf16[2,384,1536]{2,1,0:T(8,128)(2,1)} %reshape.34) | copy-start | bytes 7077892
  161.9 0.9 copy-start.6
  184.4 6.3 %copy-start = (bf16[64,16,1536]{2,1,0:T(8,128)(2,1)}, bf16[64,16,1536]{2,1,0:T(8,128)(2,1)S(1)}, u32[]{:S(2)}) copy-start(bf16[64,16,1536]{2,1,0:T(8,128)(2,1)S(1)} %all-to-all-done.1.recv_ref) | copy-start | bytes 9437188
  184.4 47.1 %all-to-all-start.2 = ((bf16[64,16,1536]{2,1,0:T(8,128)(2,1)}), bf16[64,16,1536]{2,1,0:T(8,128)(2,1)}, u32[]{:S(2)}, u32[]{:S(2)}) async-start(bf16[64,16,1536]{2,1,0:T(8,128)(2,1)} %second_mix.3), calls=%async_computation.2 | async-start | bytes 6291456 | tf_op jit(solution)/shard_map/all_to_all | solution.py:333
  190.7 55.7 %collective-permute-start.10 = (bf16[8,64,768]{2,1,0:T(8,128)(2,1)}, bf16[8,64,768]{2,1,0:T(8,128)(2,1)}, u32[]{:S(2)}, u32[]{:S(2)}) collective-permute-start(bf16[8,64,768]{2,1,0:T(8,128)(2,1)} %get-tuple-element.43), channel_id=1, source_target_pairs={{0,1},{1,0},{2,3},{3,2},{4,5},{5,4},{6,7},{7,6},{8,9},{9,8},{10,11... | collective-permute-start | bytes 2359304 | tf_op jit(solution)/shard_map/ppermute | solution.py:231
  204.5 40.9 %collective-permute-start.11 = (bf16[8,64,768]{2,1,0:T(8,128)(2,1)}, bf16[8,64,768]{2,1,0:T(8,128)(2,1)S(1)}, u32[]{:S(2)}, u32[]{:S(2)}) collective-permute-start(bf16[8,64,768]{2,1,0:T(8,128)(2,1)} %get-tuple-element.54), channel_id=1, source_target_pairs={{0,1},{1,0},{2,3},{3,2},{4,5},{5,4},{6,7},{7,6},{8,9},{9,8},{10,11... | collective-permute-start | bytes 2359304 | tf_op jit(solution)/shard_map/ppermute | solution.py:231
  219.8 41.8 %collective-permute-start.12 = (bf16[8,64,768]{2,1,0:T(8,128)(2,1)}, bf16[8,64,768]{2,1,0:T(8,128)(2,1)S(1)}, u32[]{:S(2)}, u32[]{:S(2)}) collective-permute-start(bf16[8,64,768]{2,1,0:T(8,128)(2,1)} %get-tuple-element.56), channel_id=1, source_target_pairs={{0,1},{1,0},{2,3},{3,2},{4,5},{5,4},{6,7},{7,6},{8,9},{9,8},{10,11... | collective-permute-start | bytes 2359304 | tf_op jit(solution)/shard_map/ppermute | solution.py:231
  245.4 18.8 %collective-permute-start.13 = (bf16[8,64,768]{2,1,0:T(8,128)(2,1)}, bf16[8,64,768]{2,1,0:T(8,128)(2,1)S(1)}, u32[]{:S(2)}, u32[]{:S(2)}) collective-permute-start(bf16[8,64,768]{2,1,0:T(8,128)(2,1)} %get-tuple-element.57), channel_id=1, source_target_pairs={{0,1},{1,0},{2,3},{3,2},{4,5},{5,4},{6,7},{7,6},{8,9},{9,8},{10,11... | collective-permute-start | bytes 2359304 | tf_op jit(solution)/shard_map/ppermute | solution.py:231
  260.2 20.9 %collective-permute-start.14 = (bf16[8,64,768]{2,1,0:T(8,128)(2,1)}, bf16[8,64,768]{2,1,0:T(8,128)(2,1)S(1)}, u32[]{:S(2)}, u32[]{:S(2)}) collective-permute-start(bf16[8,64,768]{2,1,0:T(8,128)(2,1)} %get-tuple-element.58), channel_id=1, source_target_pairs={{0,1},{1,0},{2,3},{3,2},{4,5},{5,4},{6,7},{7,6},{8,9},{9,8},{10,11... | collective-permute-start | bytes 2359304 | tf_op jit(solution)/shard_map/ppermute | solution.py:231
Sparse Core Ops, SparseCore 0:
  38.4 86.9 all-gather.1
